TPU v7x, 32 devices: a whole 2x2x4 slice. The times are simulated.
32 devices in a mesh: groups: 2 (over x), col: 16 (over z, y, core).
Axes of the slice: x: 2, y: 2, z: 4, core: 2. Of those that a mesh axis runs over, the one named last changes fastest.
Arguments:
- inputs: bfloat16 [64, 8192], P(('groups', 'col')), parts along dimension 0, may hold values from -6 to 6
- cotangent: bfloat16 [64, 8192], P(('groups', 'col')), parts along dimension 0, may hold values from -6 to 6
- gate_tiles: bfloat16 [192, 20, 128, 128], P('col'), may hold values from -0.15625 to 0.15625
- up_tiles: bfloat16 [192, 20, 128, 128], P('col'), may hold values from -0.15625 to 0.15625
- down_tiles: bfloat16 [192, 20, 128, 128], P('col'), may hold values from -0.078125 to 0.078125
- kept_rows: int32 [192, 20], P('col'), may hold values from 0 to 63, as said below
- kept_count: int32 [192], P('col'), may hold values from 6 to 20, as said below
Outputs:
- output: bfloat16 [64, 8192], P(('groups', 'col')), parts along dimension 0
- x_grad: bfloat16 [64, 8192], P(('groups', 'col')), parts along dimension 0
- gate_grad: bfloat16 [384, 20, 128, 128], P(('groups', 'col')), parts along dimension 0
- up_grad: bfloat16 [384, 20, 128, 128], P(('groups', 'col')), parts along dimension 0
- down_grad: bfloat16 [384, 20, 128, 128], P(('groups', 'col')), parts along dimension 0
There are 2 independent parts, one for each index of `groups`. A program takes and returns all parts, laid end to end along the dimension named above; an argument that names none is the same for every part. Nothing has to cross between parts.
Inputs may be any that keep to these rules, and one draw needn't show every extreme that they name: `kept_count`: how many slots of a column block are kept, the kept ones first; some block keeps 20, some 20 // 3. `kept_rows`: the 20 slots of a column block name different row blocks.
All inputs are finite; a program needn't handle non-finite values.
Results may differ from a plain program's by a relative error of at most 0.005.
Values may be sent and summed in bfloat16 or wider, within the bound.
No kernel may reach another device: no remote copies, remote signals or barrier semaphores. Data moves between devices by JAX's collectives and lax.ppermute only.
A program may use at most 128 MiB of HBM per device.

v0:
```python
import functools

import jax
import jax.numpy as jnp
from jax import lax
from jax.experimental import pallas as pl
from jax.experimental.pallas import tpu as pltpu
from jax.sharding import PartitionSpec as P

NT = (((1,), (1,)), ((), ()))
TN = (((0,), (0,)), ((), ()))
CHUNK = 4
STEP = 6
LAG = 2


def seed_kernel(dead, rows_ref, count_ref, x_ref, dy_ref, live_ref, block_ref, slot_ref, total_ref, x_held, dy_held):
    x_held[0] = x_ref[...]
    dy_held[0] = dy_ref[...]
    blocks, capacity = rows_ref.shape
    chunks = capacity // CHUNK

    def block(c, position):
        count = count_ref[c]
        for s in range(capacity):
            live_ref[c, s] = jnp.where(s < count, rows_ref[c, s], dead)
        for q in range(chunks):
            block_ref[position + q] = c
            slot_ref[position + q] = q * CHUNK
        return position + jnp.clip((count + CHUNK - 1) // CHUNK, 1, chunks)

    total = lax.fori_loop(0, blocks, block, 0)
    total_ref[0] = total
    for s in range(capacity):
        live_ref[blocks, s] = dead
    for i in range(STEP):
        block_ref[total + i] = blocks
        slot_ref[total + i] = 0


def add_to_rows(acc, rows, parts, blk):
    old = [acc[r] for r in rows]
    for i, r in enumerate(rows):
        acc[r] = old[i] + parts[:, i * blk : (i + 1) * blk]


def row_blocks(pad, near, far):
    half = near.shape[0]
    count, _, blk = pad.shape
    for r in range(count - 1):
        pad[r, :half] = near[:, r * blk : (r + 1) * blk]
        pad[r, half:] = far[:, r * blk : (r + 1) * blk]
    pad[count - 1] = jnp.zeros(pad.shape[1:], pad.dtype)


def layer_kernel(
    live_ref, block_ref, slot_ref, total_ref, x_near, x_far, dy_near, dy_far, wg_hbm, wu_hbm, wd_hbm,
    hidden_ref, d_ref, xpad_ref, dypad_ref, keep_ref, send_ref,
    out_acc, grad_acc, pre_acc, tiles_ref, sems,
):
    half = x_near.shape[0]
    blocks, _, capacity, blk, _ = tiles_ref.shape
    for c in range(blocks):
        for k, source in enumerate((wg_hbm, wu_hbm, wd_hbm)):
            pltpu.make_async_copy(source.at[c], tiles_ref.at[c, k], sems.at[c]).start()
    row_blocks(xpad_ref, x_near, x_far)
    row_blocks(dypad_ref, dy_near, dy_far)
    out_acc[...] = jnp.zeros_like(out_acc)
    grad_acc[...] = jnp.zeros_like(grad_acc)
    pre_acc[...] = jnp.zeros_like(pre_acc)

    def item(position):
        c, s = block_ref[position], slot_ref[position]
        rows = [live_ref[c, s + i] for i in range(CHUNK)]
        return c, s, rows, jnp.where(c < blocks, c, 0)

    def arrived(g):
        before = jnp.where(g > 0, block_ref[jnp.maximum(g * STEP - 1, 0)] + 1, 0)
        after = jnp.minimum(block_ref[g * STEP + STEP - 1] + 1, blocks)

        def wait(c, carry):
            pltpu.make_async_copy(tiles_ref.at[c], tiles_ref.at[c], sems.at[c]).wait()
            return carry

        lax.fori_loop(before, after, wait, 0)

    def gate_up_tiles(tiles, s):
        return jnp.concatenate(
            [tiles_ref[tiles, k, pl.ds(s, CHUNK)].reshape(CHUNK * blk, blk) for k in range(2)],
            axis=1,
        )

    def down_tiles(tiles, s):
        return jnp.concatenate([tiles_ref[tiles, 2, s + i] for i in range(CHUNK)], axis=1)

    def inward(position):
        c, s, rows, tiles = item(position)
        xg = jnp.concatenate([xpad_ref[r] for r in rows], axis=1)
        dyg = jnp.concatenate([dypad_ref[r] for r in rows], axis=1)
        pre = jnp.dot(xg, gate_up_tiles(tiles, s), preferred_element_type=jnp.float32)
        d_hidden = lax.dot_general(
            dyg, down_tiles(tiles, s), NT, preferred_element_type=jnp.float32
        )
        pre_acc[c, :, : 2 * blk] += pre
        pre_acc[c, :, 2 * blk :] += d_hidden

    def outward(position):
        c, s, rows, tiles = item(position)
        gate, up, d_hidden = [pre_acc[c, :, i * blk : (i + 1) * blk] for i in range(3)]
        sig = 1.0 / (1.0 + jnp.exp(-gate))
        act = gate * sig
        hidden = (act * up).astype(jnp.bfloat16)
        d_gate = (d_hidden * up * sig * (1.0 + gate * (1.0 - sig))).astype(jnp.bfloat16)
        d = jnp.concatenate([d_gate, (d_hidden * act).astype(jnp.bfloat16)], axis=1)
        hidden_ref[c] = hidden
        d_ref[c] = d
        y = jnp.dot(hidden, down_tiles(tiles, s), preferred_element_type=jnp.float32)
        x_slots = lax.dot_general(
            d, gate_up_tiles(tiles, s), NT, preferred_element_type=jnp.float32
        )
        add_to_rows(out_acc, rows, y, blk)
        add_to_rows(grad_acc, rows, x_slots, blk)

    def step(g, do_inward, do_outward):
        if do_inward:
            arrived(g)
        if do_outward:
            for i in range(STEP):
                outward((g - LAG) * STEP + i)
        if do_inward:
            for i in range(STEP):
                inward(g * STEP + i)

    steps = (total_ref[0] + STEP - 1) // STEP
    lag = jnp.minimum(steps, LAG)

    def loop(first, last, *parts):
        def body(g, carry):
            step(g, *parts)
            return carry

        lax.fori_loop(first, last, body, 0)

    loop(0, lag, True, False)
    loop(LAG, steps, True, True)
    loop(steps - lag + LAG, steps + LAG, False, True)
    for r in range(out_acc.shape[0] - 1):
        columns = slice(r * blk, (r + 1) * blk)
        for i, acc in enumerate((out_acc, grad_acc)):
            keep_ref[i, :, columns] = acc[r, :half]
            send_ref[i, :, columns] = acc[r, half:].astype(send_ref.dtype)


def gate_up_products(pad_ref, d, rows, slots, blk, stages, i):
    for s in slots[::2]:
        xs = jnp.concatenate([pad_ref[r] for r in rows[s : s + 2]], axis=1)
        full = lax.dot_general(xs, d, TN, preferred_element_type=jnp.float32)
        full = full.astype(jnp.bfloat16)
        for k in range(2):
            stages[0][i, s + k] = full[k * blk : (k + 1) * blk, :blk]
            stages[1][i, s + k] = full[k * blk : (k + 1) * blk, blk:]


def down_products(pad_ref, hidden, rows, slots, blk, stages, i):
    for s in slots[::CHUNK]:
        dys = jnp.concatenate([pad_ref[r] for r in rows[s : s + CHUNK]], axis=1)
        full = lax.dot_general(hidden, dys, TN, preferred_element_type=jnp.float32)
        full = full.astype(jnp.bfloat16)
        for k in range(CHUNK):
            stages[0][i, s + k] = full[:, k * blk : (k + 1) * blk]


def grad_kernel(products, first, count, outs, behind, *refs):
    live_ref, pad_ref, factor_ref = refs[:3]
    grad_refs = refs[3 + behind : 3 + behind + outs]
    stages = refs[3 + behind + outs : -1]
    sems = refs[-1]
    capacity, blk = stages[0].shape[1], stages[0].shape[-1]
    cut = capacity // 2 // CHUNK * CHUNK
    parts = (range(cut), range(cut, capacity))

    def copies(i, h):
        part = pl.ds(parts[h].start, len(parts[h]))
        return [
            pltpu.make_async_copy(stage.at[i, part], grad.at[first + i, part], sems.at[k, i, h])
            for k, (stage, grad) in enumerate(zip(stages, grad_refs))
        ]

    group = max(k for k in range(1, 5) if count % k == 0)

    def step(g, carry):
        some = [g * group + k for k in range(group)]
        rows = [[live_ref[first + i, s] for s in range(capacity)] for i in some]
        for i, names in zip(some, rows):
            for h in range(2):
                products(pad_ref, factor_ref[first + i], names, parts[h], blk, stages, i)
                for copy in copies(i, h):
                    copy.start()
        return carry

    lax.fori_loop(0, count // group, step, 0)
    for i in range(count):
        for h in range(2):
            for copy in copies(i, h):
                copy.wait()


def hop_orders(n):
    bits = [1 << i for i in range(n.bit_length() - 2, 0, -1)]
    return bits, bits[:-2] + bits[:-3:-1]


def swap(value, bits, n):
    return lax.ppermute(value, "col", [(j, j ^ bits[j % 2]) for j in range(n)])


def gather_hops(held, value, hops, n):
    send = value[None]
    for i, bits in enumerate(hops):
        if i:
            send = held[: 1 << i]
        held = lax.dynamic_update_slice_in_dim(held, swap(send, bits, n), 1 << i, 0)
    return held


def rows_of(held, swapped):
    pieces, mine, width = held.shape
    if swapped:
        held = held.reshape(2, 2, pieces // 4, mine, width).transpose(1, 0, 2, 3, 4)
    return held.reshape(pieces * mine, width)


def local(n, inputs, cotangent, gate_tiles, up_tiles, down_tiles, kept_rows, kept_count):
    blocks, capacity, blk, _ = gate_tiles.shape
    mine, width = inputs.shape
    tokens = mine * n
    smem = pl.BlockSpec(memory_space=pltpu.SMEM)
    vmem = pl.BlockSpec(memory_space=pltpu.VMEM)
    hbm = pl.BlockSpec(memory_space=pltpu.HBM)
    tile_bytes = blocks * capacity * blk * blk * 2
    tiles_in = [
        pltpu.with_memory_space_constraint(t, pltpu.HBM) for t in (gate_tiles, up_tiles, down_tiles)
    ]

    def cost(products, tiles, part=1.0):
        return pl.CostEstimate(
            flops=int(products * tokens * tile_bytes * part),
            bytes_accessed=int(tiles * tile_bytes * part),
            transcendentals=0,
        )

    listed = pltpu.SMEM((blocks * (capacity // CHUNK) + capacity // CHUNK + STEP,), jnp.int32)
    live, item_block, item_slot, total, x_held, dy_held = pl.pallas_call(
        functools.partial(seed_kernel, width // blk),
        in_specs=[smem, smem, vmem, vmem],
        out_specs=[smem] * 4 + [vmem] * 2,
        out_shape=[
            pltpu.SMEM((blocks + 1, capacity), jnp.int32),
            listed,
            listed,
            pltpu.SMEM((1,), jnp.int32),
        ]
        + [pltpu.VMEM((n // 2, mine, width), inputs.dtype)] * 2,
        name="seed",
    )(kept_rows, kept_count, inputs, cotangent)
    cores = (1, 1)
    first, second = hop_orders(n)
    x_hops, dy_hops = list(zip(first, second)), list(zip(second, first))
    x_held = gather_hops(x_held, inputs, x_hops, n)
    dy_held = gather_hops(dy_held, cotangent, dy_hops, n)
    x_near, x_far = [rows_of(v, False) for v in (x_held, swap(x_held, cores, n))]
    dy_near, dy_far = [rows_of(v, True) for v in (dy_held, swap(dy_held, cores, n))]

    padded = pltpu.VMEM((width // blk + 1, tokens, blk), jnp.bfloat16)
    acc = pltpu.VMEM((width // blk + 1, tokens, blk), jnp.float32)
    hidden, d, xpad, dypad, keep, send = pl.pallas_call(
        layer_kernel,
        in_specs=[smem] * 4 + [vmem] * 4 + [hbm] * 3,
        out_specs=[vmem] * 6,
        out_shape=[
            pltpu.VMEM((blocks + 1, tokens, blk), jnp.bfloat16),
            pltpu.VMEM((blocks + 1, tokens, 2 * blk), jnp.bfloat16),
            padded,
            padded,
            pltpu.VMEM((2, tokens // 2, width), jnp.float32),
            pltpu.VMEM((2, tokens // 2, width), jnp.bfloat16),
        ],
        scratch_shapes=[acc, acc, pltpu.VMEM((blocks + 1, tokens, 3 * blk), jnp.float32)]
        + [
            pltpu.VMEM((blocks, 3) + gate_tiles.shape[1:], jnp.bfloat16),
            pltpu.SemaphoreType.DMA((blocks,)),
        ],
        compiler_params=pltpu.CompilerParams(vmem_limit_bytes=40 * 1024 * 1024),
        cost_estimate=cost(6, 3),
        name="layer",
    )(live, item_block, item_slot, total, x_near, x_far, dy_near, dy_far, *tiles_in)

    def grads(products, pad, factor, first, count, outs, earlier, after, name):
        behind = len(earlier) + len(after)
        return pl.pallas_call(
            functools.partial(grad_kernel, products, first, count, outs, behind),
            in_specs=[smem, vmem, vmem]
            + [hbm] * len(earlier)
            + [pl.BlockSpec(memory_space=pl.ANY)] * len(after),
            out_specs=[hbm] * outs,
            out_shape=[jax.ShapeDtypeStruct(gate_tiles.shape, jnp.bfloat16)] * outs,
            scratch_shapes=[pltpu.VMEM((count,) + gate_tiles.shape[1:], jnp.bfloat16)] * outs
            + [pltpu.SemaphoreType.DMA((outs, count, 2))],
            input_output_aliases={3 + k: k for k in range(len(earlier))},
            compiler_params=pltpu.CompilerParams(vmem_limit_bytes=24 * 1024 * 1024),
            cost_estimate=cost(outs, outs, count / blocks),
            name=name,
        )(live, pad, factor, *earlier, *after)

    third = -(-blocks // 3)
    cuts = {0: (0, third), 2: (third, 2 * third), 3: (2 * third, blocks)}
    gate_up, down_grad, after = [], None, []
    for i, bits in enumerate([cores] + x_hops[::-1]):
        got = swap(send, bits, n)
        done = []
        if i == 1:
            (down_grad,) = grads(
                down_products, dypad, hidden, 0, blocks, 1, [], after, "down_grad"
            )
            done = [down_grad]
        elif i in cuts:
            first, last = cuts[i]
            gate_up = grads(
                gate_up_products, xpad, d, first, last - first, 2, gate_up, after, "gate_up_grad"
            )
            done = gate_up
        total = keep + got.astype(jnp.float32)
        if i < len(x_hops):
            half = total.shape[1] // 2
            keep, send = total[:, :half], total[:, half:].astype(jnp.bfloat16)
            send, done = lax.optimization_barrier((send, done))
            after = [send]
            if i == 1:
                (down_grad,) = done
            elif i in cuts:
                gate_up = done
    total = total.astype(jnp.bfloat16)
    return total[0], total[1], gate_up[0], gate_up[1], down_grad


def solution(mesh):
    tiles = P("col", None, None, None)
    tokens = P(("groups", "col"), None)
    grads = P(("groups", "col"), None, None, None)
    return jax.shard_map(
        functools.partial(local, mesh.shape["col"]),
        mesh=mesh,
        in_specs=(tokens, tokens, tiles, tiles, tiles, P("col", None), P("col")),
        out_specs=(tokens, tokens, grads, grads, grads),
        check_vma=False,
    )
```

profile of v0, /device:TPU:0, one launch (start us, length us, event | category | flops | bytes accessed | tf_op | source)
XLA Modules:
  0.0 56.0 jit_solution(5891379584762582308)
XLA Ops:
  0.6 4.1 %collective-permute-start.4 = (bf16[1,2,8192]{2,1,0:T(2,128)(2,1)}, bf16[1,2,8192]{2,1,0:T(2,128)(2,1)S(1)}, u32[]{:S(2)}, u32[]{:S(2)}) collective-permute-start(bf16[1,2,8192]{2,1,0:T(2,128)(2,1)} %bitcast.18), channel_id=1, source_target_pairs={{0,8},{1,9},{2,10},{3,11},{4,12},{5,13},{6,14},{7,15},{8,0},{9,1},... | collective-permute-start | bytes 98312 | tf_op jit(solution)/shard_map/ppermute | solution.py:214
  4.8 1.4 %seed.1 = (s32[13,20]{1,0:T(8,128)S(4)}, s32[71]{0:T(128)S(4)}, s32[71]{0:T(128)S(4)}, s32[1]{0:T(128)S(4)}, bf16[8,2,8192]{2,1,0:T(2,128)(2,1)S(1)}, /*index=5*/bf16[8,2,8192]{2,1,0:T(2,128)(2,1)S(1)}) custom-call(s32[12,20]{1,0:T(8,128)} %rows_ref.1, s32[12]{0:T(128)} %count_ref.1, bf16[2,8192]{1,0:T(2,128)(2,1)} %x_ref.1, bf16[2,8192]{1,0:T(2,128)(2,1)} %dy_ref.1), custom_call_target="tpu_custom_call" | custom-call | tf_op jit(solution)/shard_map/seed/pallas_call | solution.py:253
  6.2 1.0 %collective-permute-done.4 = bf16[1,2,8192]{2,1,0:T(2,128)(2,1)S(1)} collective-permute-done((bf16[1,2,8192]{2,1,0:T(2,128)(2,1)}, bf16[1,2,8192]{2,1,0:T(2,128)(2,1)S(1)}, u32[]{:S(2)}, u32[]{:S(2)}) %collective-permute-start.4) | collective-permute-done | bytes 32800 | tf_op jit(solution)/shard_map/ppermute | solution.py:214
  7.3 1.8 %collective-permute-start.5 = (bf16[2,2,8192]{2,1,0:T(2,128)(2,1)S(1)}, bf16[2,2,8192]{2,1,0:T(2,128)(2,1)S(1)}, u32[]{:S(2)}, u32[]{:S(2)}) collective-permute-start(bf16[2,2,8192]{2,1,0:T(2,128)(2,1)S(1)} %slice.53), channel_id=1, source_target_pairs={{0,2},{1,5},{2,0},{3,7},{4,6},{5,1},{6,4},{7,3},{8,10},{9,13},{10,... | collective-permute-start | bytes 196616 | tf_op jit(solution)/shard_map/ppermute | solution.py:214
  9.1 0.7 %collective-permute-done = bf16[1,2,8192]{2,1,0:T(2,128)(2,1)S(1)} collective-permute-done((bf16[1,2,8192]{2,1,0:T(2,128)(2,1)}, bf16[1,2,8192]{2,1,0:T(2,128)(2,1)S(1)}, u32[]{:S(2)}, u32[]{:S(2)}) %collective-permute-start) | collective-permute-done | bytes 32800 | tf_op jit(solution)/shard_map/ppermute | solution.py:214
  9.8 1.6 %collective-permute-start.1 = (bf16[2,2,8192]{2,1,0:T(2,128)(2,1)S(1)}, bf16[2,2,8192]{2,1,0:T(2,128)(2,1)S(1)}, u32[]{:S(2)}, u32[]{:S(2)}) collective-permute-start(bf16[2,2,8192]{2,1,0:T(2,128)(2,1)S(1)} %slice.51), channel_id=1, source_target_pairs={{0,4},{1,3},{2,6},{3,1},{4,0},{5,7},{6,2},{7,5},{8,12},{9,11},{10,... | collective-permute-start | bytes 196616 | tf_op jit(solution)/shard_map/ppermute | solution.py:214
  11.5 0.6 %collective-permute-done.5 = bf16[2,2,8192]{2,1,0:T(2,128)(2,1)S(1)} collective-permute-done((bf16[2,2,8192]{2,1,0:T(2,128)(2,1)S(1)}, bf16[2,2,8192]{2,1,0:T(2,128)(2,1)S(1)}, u32[]{:S(2)}, u32[]{:S(2)}) %collective-permute-start.5) | collective-permute-done | bytes 65568 | tf_op jit(solution)/shard_map/ppermute | solution.py:214
  12.3 1.8 %collective-permute-start.6 = (bf16[4,2,8192]{2,1,0:T(2,128)(2,1)S(1)}, bf16[4,2,8192]{2,1,0:T(2,128)(2,1)S(1)}, u32[]{:S(2)}, u32[]{:S(2)}) collective-permute-start(bf16[4,2,8192]{2,1,0:T(2,128)(2,1)S(1)} %slice.54), channel_id=1, source_target_pairs={{0,4},{1,3},{2,6},{3,1},{4,0},{5,7},{6,2},{7,5},{8,12},{9,11},{10,... | collective-permute-start | bytes 393224 | tf_op jit(solution)/shard_map/ppermute | solution.py:214
  14.3 1.6 %collective-permute-start.2 = (bf16[4,2,8192]{2,1,0:T(2,128)(2,1)S(1)}, bf16[4,2,8192]{2,1,0:T(2,128)(2,1)S(1)}, u32[]{:S(2)}, u32[]{:S(2)}) collective-permute-start(bf16[4,2,8192]{2,1,0:T(2,128)(2,1)S(1)} %slice.52), channel_id=1, source_target_pairs={{0,2},{1,5},{2,0},{3,7},{4,6},{5,1},{6,4},{7,3},{8,10},{9,13},{10,... | collective-permute-start | bytes 393224 | tf_op jit(solution)/shard_map/ppermute | solution.py:214
  15.9 1.9 %collective-permute-done.6 = bf16[4,2,8192]{2,1,0:T(2,128)(2,1)S(1)} collective-permute-done((bf16[4,2,8192]{2,1,0:T(2,128)(2,1)S(1)}, bf16[4,2,8192]{2,1,0:T(2,128)(2,1)S(1)}, u32[]{:S(2)}, u32[]{:S(2)}) %collective-permute-start.6) | collective-permute-done | bytes 131104 | tf_op jit(solution)/shard_map/ppermute | solution.py:214
  17.9 0.1 constant_dynamic-update-slice_fusion
  18.0 1.3 %collective-permute-done.2 = bf16[4,2,8192]{2,1,0:T(2,128)(2,1)S(1)} collective-permute-done((bf16[4,2,8192]{2,1,0:T(2,128)(2,1)S(1)}, bf16[4,2,8192]{2,1,0:T(2,128)(2,1)S(1)}, u32[]{:S(2)}, u32[]{:S(2)}) %collective-permute-start.2) | collective-permute-done | bytes 131104 | tf_op jit(solution)/shard_map/ppermute | solution.py:214
  19.4 0.1 constant_dynamic-update-slice_fusion.3
  19.6 0.1 reshape.28.x_near
  19.7 0.2 copy.21
  19.9 0.1 reshape.31.dy_near
  20.0 0.2 copy.20
  20.2 0.1 reshape.33.dy_far
  20.3 0.8 %collective-permute-done.3 = bf16[8,2,8192]{2,1,0:T(2,128)(2,1)S(1)} collective-permute-done((bf16[8,2,8192]{2,1,0:T(2,128)(2,1)S(1)}, bf16[8,2,8192]{2,1,0:T(2,128)(2,1)S(1)}, u32[]{:S(2)}, u32[]{:S(2)}) %collective-permute-start.3) | collective-permute-done | bytes 262176 | tf_op jit(solution)/shard_map/ppermute | solution.py:214
  21.2 12.3 %layer.1 = (bf16[13,32,128]{2,1,0:T(8,128)(2,1)S(1)}, bf16[13,32,256]{2,1,0:T(8,128)(2,1)S(1)}, bf16[65,32,128]{2,1,0:T(8,128)(2,1)S(1)}, bf16[65,32,128]{2,1,0:...) custom-call(s32[13,20]{1,0:T(8,128)S(4)} %get-tuple-element.31.live_ref.refs_0_, ...), custom_call_target="tpu_custom_call" | custom-call | flops 1509949440 | bytes 23592960 | tf_op jit(solution)/shard_map/layer/pallas_call | solution.py:276
  33.5 0.7 %collective-permute-start.8 = (bf16[2,16,8192]{2,1,0:T(8,128)(2,1)S(1)}, bf16[2,16,8192]{2,1,0:T(8,128)(2,1)S(1)}, u32[]{:S(2)}, u32[]{:S(2)}) collective-permute-start(bf16[2,16,8192]{2,1,0:T(8,128)(2,1)S(1)} %get-tuple-element.38), channel_id=1, source_target_pairs={{0,1},{1,0},{2,3},{3,2},{4,5},{5,4},{6,7},{7,6},{8,9},{9,8},{10,11... | collective-permute-start | bytes 1572872 | tf_op jit(solution)/shard_map/ppermute | solution.py:214
  34.2 2.8 %gate_up_grad.3 = (bf16[12,20,128,128]{3,2,1,0:T(8,128)(2,1)}, bf16[12,20,128,128]{3,2,1,0:T(8,128)(2,1)}) custom-call(s32[13,20]{1,0:T(8,128)S(4)} %get-tuple-element.31.live_ref.refs_0_, bf16[65,32,128]{2,1,0:T(8,128)(2,1)S(1)} %get-tuple-element.39.refs_1_, bf16[13,32,256]{2,1,0:T(8,128)(2,1)S(1)} %get-tuple-element.40.refs_2_), custom_call_target="tpu_custom_call" | custom-call | flops 167772160 | bytes 5242880 | tf_op jit(solution)/shard_map/gate_up_grad/pallas_call | solution.py:300
  37.2 3.2 %collective-permute-start.9 = (bf16[2,8,8192]{2,1,0:T(8,128)(2,1)S(1)}, bf16[2,8,8192]{2,1,0:T(8,128)(2,1)S(1)}, u32[]{:S(2)}, u32[]{:S(2)}) collective-permute-start(bf16[2,8,8192]{2,1,0:T(8,128)(2,1)S(1)} %slice.73.refs_3_), channel_id=1, source_target_pairs={{0,2},{1,5},{2,0},{3,7},{4,6},{5,1},{6,4},{7,3},{8,10},{9,13},{10,... | collective-permute-start | bytes 786440 | tf_op jit(solution)/shard_map/ppermute | solution.py:214
  40.4 3.6 %down_grad.1 = bf16[12,20,128,128]{3,2,1,0:T(8,128)(2,1)} custom-call(s32[13,20]{1,0:T(8,128)S(4)} %get-tuple-element.31.live_ref.refs_0_, bf16[65,32,128]{2,1,0:T(8,128)(2,1)S(1)} %get-tuple-element.44.refs_1_, bf16[13,32,128]{2,1,0:T(8,128)(2,1)S(1)} %get-tuple-element.45.refs_2_, bf16[2,8,8192]{2,1,0:T(8,128)(2,1)S(1)} %slice.73.refs_3_), custom_call_target="tpu_custom_call" | custom-call | flops 251658240 | bytes 7864320 | tf_op jit(solution)/shard_map/down_grad/pallas_call | solution.py:300
  44.0 0.7 %collective-permute-done.9 = bf16[2,8,8192]{2,1,0:T(8,128)(2,1)S(1)} collective-permute-done((bf16[2,8,8192]{2,1,0:T(8,128)(2,1)S(1)}, bf16[2,8,8192]{2,1,0:T(8,128)(2,1)S(1)}, u32[]{:S(2)}, u32[]{:S(2)}) %collective-permute-start.9) | collective-permute-done | bytes 262176 | tf_op jit(solution)/shard_map/ppermute | solution.py:214
  44.9 1.5 %collective-permute-start.10 = (bf16[2,4,8192]{2,1,0:T(4,128)(2,1)S(1)}, bf16[2,4,8192]{2,1,0:T(4,128)(2,1)S(1)}, u32[]{:S(2)}, u32[]{:S(2)}) collective-permute-start(bf16[2,4,8192]{2,1,0:T(4,128)(2,1)S(1)} %slice.74.refs_5_), channel_id=1, source_target_pairs={{0,4},{1,3},{2,6},{3,1},{4,0},{5,7},{6,2},{7,5},{8,12},{9,11},{10,... | collective-permute-start | bytes 393224 | tf_op jit(solution)/shard_map/ppermute | solution.py:214
  46.4 2.8 %gate_up_grad.4 = (bf16[12,20,128,128]{3,2,1,0:T(8,128)(2,1)}, bf16[12,20,128,128]{3,2,1,0:T(8,128)(2,1)}) custom-call(s32[13,20]{1,0:T(8,128)S(4)} %get-tuple-element.31.live_ref.refs_0_, bf16[65,32,128]{2,1,0:T(8,128)(2,1)S(1)} %get-tuple-element.39.refs_1_, ...), custom_call_target="tpu_custom_call", output_to_operand_aliasing={{0}: (3, {}), {1}: (4, {})} | custom-call | flops 167772160 | bytes 5242880 | tf_op jit(solution)/shard_map/gate_up_grad/pallas_call | solution.py:300
  49.3 0.6 %collective-permute-done.10 = bf16[2,4,8192]{2,1,0:T(4,128)(2,1)S(1)} collective-permute-done((bf16[2,4,8192]{2,1,0:T(4,128)(2,1)S(1)}, bf16[2,4,8192]{2,1,0:T(4,128)(2,1)S(1)}, u32[]{:S(2)}, u32[]{:S(2)}) %collective-permute-start.10) | collective-permute-done | bytes 131104 | tf_op jit(solution)/shard_map/ppermute | solution.py:214
  50.0 2.0 %collective-permute-start.11 = (bf16[2,2,8192]{2,1,0:T(2,128)(2,1)S(1)}, bf16[2,2,8192]{2,1,0:T(2,128)(2,1)S(1)}, u32[]{:S(2)}, u32[]{:S(2)}) collective-permute-start(bf16[2,2,8192]{2,1,0:T(2,128)(2,1)S(1)} %slice.75.refs_5_), channel_id=1, source_target_pairs={{0,8},{1,9},{2,10},{3,11},{4,12},{5,13},{6,14},{7,15},{8,0},{9,1},... | collective-permute-start | bytes 196616 | tf_op jit(solution)/shard_map/ppermute | solution.py:214
  52.0 2.8 %gate_up_grad.5 = (bf16[12,20,128,128]{3,2,1,0:T(8,128)(2,1)}, bf16[12,20,128,128]{3,2,1,0:T(8,128)(2,1)}) custom-call(s32[13,20]{1,0:T(8,128)S(4)} %get-tuple-element.31.live_ref.refs_0_, bf16[65,32,128]{2,1,0:T(8,128)(2,1)S(1)} %get-tuple-element.39.refs_1_, ...), custom_call_target="tpu_custom_call", output_to_operand_aliasing={{0}: (3, {}), {1}: (4, {})} | custom-call | flops 167772160 | bytes 5242880 | tf_op jit(solution)/shard_map/gate_up_grad/pallas_call | solution.py:300
  54.9 0.4 collective-permute-done.11
  55.4 0.7 %slice_bitcast_fusion = (bf16[2,8192]{1,0:T(2,128)(2,1)}, bf16[2,8192]{1,0:T(2,128)(2,1)}) fusion(bf16[2,2,8192]{2,1,0:T(2,128)(2,1)S(1)} %fusion), kind=kLoop, calls=%fused_computation.10 | loop fusion | bytes 131072 | tf_op jit(solution)/shard_map/squeeze | solution.py:343
  (22 shorter events, 1.3 us)
Async XLA Ops:
  0.6 6.6 %collective-permute-start.4 = (bf16[1,2,8192]{2,1,0:T(2,128)(2,1)}, bf16[1,2,8192]{2,1,0:T(2,128)(2,1)S(1)}, u32[]{:S(2)}, u32[]{:S(2)}) collective-permute-start(bf16[1,2,8192]{2,1,0:T(2,128)(2,1)} %bitcast.18), channel_id=1, source_target_pairs={{0,8},{1,9},{2,10},{3,11},{4,12},{5,13},{6,14},{7,15},{8,0},{9,1},... | collective-permute-start | bytes 98312 | tf_op jit(solution)/shard_map/ppermute | solution.py:214
  4.7 5.0 %collective-permute-start = (bf16[1,2,8192]{2,1,0:T(2,128)(2,1)}, bf16[1,2,8192]{2,1,0:T(2,128)(2,1)S(1)}, u32[]{:S(2)}, u32[]{:S(2)}) collective-permute-start(bf16[1,2,8192]{2,1,0:T(2,128)(2,1)} %bitcast.19), channel_id=1, source_target_pairs={{0,8},{1,9},{2,10},{3,11},{4,12},{5,13},{6,14},{7,15},{8,0},{9,1},... | collective-permute-start | bytes 98312 | tf_op jit(solution)/shard_map/ppermute | solution.py:214
  7.3 4.8 %collective-permute-start.5 = (bf16[2,2,8192]{2,1,0:T(2,128)(2,1)S(1)}, bf16[2,2,8192]{2,1,0:T(2,128)(2,1)S(1)}, u32[]{:S(2)}, u32[]{:S(2)}) collective-permute-start(bf16[2,2,8192]{2,1,0:T(2,128)(2,1)S(1)} %slice.53), channel_id=1, source_target_pairs={{0,2},{1,5},{2,0},{3,7},{4,6},{5,1},{6,4},{7,3},{8,10},{9,13},{10,... | collective-permute-start | bytes 196616 | tf_op jit(solution)/shard_map/ppermute | solution.py:214
  9.8 4.3 %collective-permute-start.1 = (bf16[2,2,8192]{2,1,0:T(2,128)(2,1)S(1)}, bf16[2,2,8192]{2,1,0:T(2,128)(2,1)S(1)}, u32[]{:S(2)}, u32[]{:S(2)}) collective-permute-start(bf16[2,2,8192]{2,1,0:T(2,128)(2,1)S(1)} %slice.51), channel_id=1, source_target_pairs={{0,4},{1,3},{2,6},{3,1},{4,0},{5,7},{6,2},{7,5},{8,12},{9,11},{10,... | collective-permute-start | bytes 196616 | tf_op jit(solution)/shard_map/ppermute | solution.py:214
  12.3 5.6 %collective-permute-start.6 = (bf16[4,2,8192]{2,1,0:T(2,128)(2,1)S(1)}, bf16[4,2,8192]{2,1,0:T(2,128)(2,1)S(1)}, u32[]{:S(2)}, u32[]{:S(2)}) collective-permute-start(bf16[4,2,8192]{2,1,0:T(2,128)(2,1)S(1)} %slice.54), channel_id=1, source_target_pairs={{0,4},{1,3},{2,6},{3,1},{4,0},{5,7},{6,2},{7,5},{8,12},{9,11},{10,... | collective-permute-start | bytes 393224 | tf_op jit(solution)/shard_map/ppermute | solution.py:214
  14.3 5.0 %collective-permute-start.2 = (bf16[4,2,8192]{2,1,0:T(2,128)(2,1)S(1)}, bf16[4,2,8192]{2,1,0:T(2,128)(2,1)S(1)}, u32[]{:S(2)}, u32[]{:S(2)}) collective-permute-start(bf16[4,2,8192]{2,1,0:T(2,128)(2,1)S(1)} %slice.52), channel_id=1, source_target_pairs={{0,2},{1,5},{2,0},{3,7},{4,6},{5,1},{6,4},{7,3},{8,10},{9,13},{10,... | collective-permute-start | bytes 393224 | tf_op jit(solution)/shard_map/ppermute | solution.py:214
  18.0 2.0 %collective-permute-start.7 = (bf16[8,2,8192]{2,1,0:T(2,128)(2,1)S(1)}, bf16[8,2,8192]{2,1,0:T(2,128)(2,1)S(1)}, u32[]{:S(2)}, u32[]{:S(2)}) collective-permute-start(bf16[8,2,8192]{2,1,0:T(2,128)(2,1)S(1)} %constant_dynamic-update-slice_fusion), channel_id=1, source_target_pairs={{0,1},{1,0},{2,3},{3,2},{4,5},{5,4},{6,7},{7,6},{8,9},{9,8},{10,11... | collective-permute-start | bytes 786440 | tf_op jit(solution)/shard_map/ppermute | solution.py:214
  19.5 1.6 %collective-permute-start.3 = (bf16[8,2,8192]{2,1,0:T(2,128)(2,1)S(1)}, bf16[8,2,8192]{2,1,0:T(2,128)(2,1)S(1)}, u32[]{:S(2)}, u32[]{:S(2)}) collective-permute-start(bf16[8,2,8192]{2,1,0:T(2,128)(2,1)S(1)} %constant_dynamic-update-slice_fusion.3), channel_id=1, source_target_pairs={{0,1},{1,0},{2,3},{3,2},{4,5},{5,4},{6,7},{7,6},{8,9},{9,8},{10,11... | collective-permute-start | bytes 786440 | tf_op jit(solution)/shard_map/ppermute | solution.py:214
  33.5 3.5 %collective-permute-start.8 = (bf16[2,16,8192]{2,1,0:T(8,128)(2,1)S(1)}, bf16[2,16,8192]{2,1,0:T(8,128)(2,1)S(1)}, u32[]{:S(2)}, u32[]{:S(2)}) collective-permute-start(bf16[2,16,8192]{2,1,0:T(8,128)(2,1)S(1)} %get-tuple-element.38), channel_id=1, source_target_pairs={{0,1},{1,0},{2,3},{3,2},{4,5},{5,4},{6,7},{7,6},{8,9},{9,8},{10,11... | collective-permute-start | bytes 1572872 | tf_op jit(solution)/shard_map/ppermute | solution.py:214
  37.2 7.6 %collective-permute-start.9 = (bf16[2,8,8192]{2,1,0:T(8,128)(2,1)S(1)}, bf16[2,8,8192]{2,1,0:T(8,128)(2,1)S(1)}, u32[]{:S(2)}, u32[]{:S(2)}) collective-permute-start(bf16[2,8,8192]{2,1,0:T(8,128)(2,1)S(1)} %slice.73.refs_3_), channel_id=1, source_target_pairs={{0,2},{1,5},{2,0},{3,7},{4,6},{5,1},{6,4},{7,3},{8,10},{9,13},{10,... | collective-permute-start | bytes 786440 | tf_op jit(solution)/shard_map/ppermute | solution.py:214
  44.9 5.0 %collective-permute-start.10 = (bf16[2,4,8192]{2,1,0:T(4,128)(2,1)S(1)}, bf16[2,4,8192]{2,1,0:T(4,128)(2,1)S(1)}, u32[]{:S(2)}, u32[]{:S(2)}) collective-permute-start(bf16[2,4,8192]{2,1,0:T(4,128)(2,1)S(1)} %slice.74.refs_5_), channel_id=1, source_target_pairs={{0,4},{1,3},{2,6},{3,1},{4,0},{5,7},{6,2},{7,5},{8,12},{9,11},{10,... | collective-permute-start | bytes 393224 | tf_op jit(solution)/shard_map/ppermute | solution.py:214
  50.0 5.2 %collective-permute-start.11 = (bf16[2,2,8192]{2,1,0:T(2,128)(2,1)S(1)}, bf16[2,2,8192]{2,1,0:T(2,128)(2,1)S(1)}, u32[]{:S(2)}, u32[]{:S(2)}) collective-permute-start(bf16[2,2,8192]{2,1,0:T(2,128)(2,1)S(1)} %slice.75.refs_5_), channel_id=1, source_target_pairs={{0,8},{1,9},{2,10},{3,11},{4,12},{5,13},{6,14},{7,15},{8,0},{9,1},... | collective-permute-start | bytes 196616 | tf_op jit(solution)/shard_map/ppermute | solution.py:214
where the time goes:
time: 56.3 us; the launch traced here: 56 us
  Pallas kernels  25.9 us (46%)
  starting transfers between devices  18.6 us (33%)
  waiting for transfers between devices  8.17 us (15%)
  local copies, waits for them, and re-layouts  2.28 us (4%)
  between operations  0.84 us (1%)
    ppermute x12, starting transfers between devices, swap(): return lax.ppermute(value, 'col', [(j, j ^ bits[j % 2]) for j in range(n)])  18.6 us
    pallas_call x1, Pallas kernels, local(): pl.pallas_call(layer_kernel, in_specs=[smem] * 4 + [vmem] * 4 + [hbm] * 3...  12.3 us
    pallas_call x4, Pallas kernels, grads(): pl.pallas_call(functools.partial(grad_kernel, products, first, count, out...  12.1 us
    ppermute x12, waiting for transfers between devices, swap(): return lax.ppermute(value, 'col', [(j, j ^ bits[j % 2]) for j in range(n)])  8.17 us
    pallas_call x1, Pallas kernels, local(): pl.pallas_call(functools.partial(seed_kernel, width // blk), in_specs=[sm...  1.42 us
  transfers between devices with their start and end apart: 12, of which 10 were waited for; matrix products, arithmetic and copies ran while one was open for 2% of the time, Pallas kernels for 24%

commit v1 on v0

--- a/solution.py
+++ b/solution.py
@@ -10,7 +10,7 @@
 NT = (((1,), (1,)), ((), ()))
 TN = (((0,), (0,)), ((), ()))
 CHUNK = 4
-STEP = 6
+STEP = 4
 LAG = 2
 
 
@@ -115,9 +115,8 @@
         hidden_ref[c] = hidden
         d_ref[c] = d
         y = jnp.dot(hidden, down_tiles(tiles, s), preferred_element_type=jnp.float32)
-        x_slots = lax.dot_general(
-            d, gate_up_tiles(tiles, s), NT, preferred_element_type=jnp.float32
-        )
+        turned = jnp.dot(gate_up_tiles(tiles, s), d.T, preferred_element_type=jnp.float32)
+        x_slots = turned.T
         add_to_rows(out_acc, rows, y, blk)
         add_to_rows(grad_acc, rows, x_slots, blk)
 

time: 56.3 us -> 55.8 us (level)
  starting transfers between devices: 18.6 us -> 17 us
  waiting for transfers between devices: 8.17 us -> 8.83 us
    ppermute x12, starting transfers between devices: 18.6 us -> 17 us  [swap(): return lax.ppermute(value, 'col', [(j, j ^ bits[j % 2]) for j in range(n)])]
    ppermute x12, waiting for transfers between devices: 8.17 us -> 8.83 us  [swap(): return lax.ppermute(value, 'col', [(j, j ^ bits[j % 2]) for j in range(n)])]
  transfers between devices with their start and end apart: 12 -> 12, of which waited for: 10 -> 10; matrix products, arithmetic and copies ran while one was open for 2% -> 2% of each run, Pallas kernels for 24% -> 25%
where the time goes in v1:
time: 55.8 us; the launch traced here: 55.2 us
  Pallas kernels  26 us (47%)
  starting transfers between devices  17 us (30%)
  waiting for transfers between devices  8.83 us (16%)
  local copies, waits for them, and re-layouts  2.28 us (4%)
  between operations  0.84 us (2%)
    ppermute x12, starting transfers between devices, swap(): return lax.ppermute(value, 'col', [(j, j ^ bits[j % 2]) for j in range(n)])  17 us
    pallas_call x1, Pallas kernels, local(): pl.pallas_call(layer_kernel, in_specs=[smem] * 4 + [vmem] * 4 + [hbm] * 3...  12.5 us
    pallas_call x4, Pallas kernels, grads(): pl.pallas_call(functools.partial(grad_kernel, products, first, count, out...  12.1 us
    ppermute x12, waiting for transfers between devices, swap(): return lax.ppermute(value, 'col', [(j, j ^ bits[j % 2]) for j in range(n)])  8.83 us
    pallas_call x1, Pallas kernels, local(): pl.pallas_call(functools.partial(seed_kernel, width // blk), in_specs=[sm...  1.41 us
  transfers between devices with their start and end apart: 12, of which 10 were waited for; matrix products, arithmetic and copies ran while one was open for 2% of the time, Pallas kernels for 25%

profile of v1, /device:TPU:0, one launch (start us, length us, event | category | flops | bytes accessed | tf_op | source)
XLA Modules:
  0.0 55.2 jit_solution(5377651229562193713)
XLA Ops:
  0.6 4.1 %collective-permute-start.4 = (bf16[1,2,8192]{2,1,0:T(2,128)(2,1)}, bf16[1,2,8192]{2,1,0:T(2,128)(2,1)S(1)}, u32[]{:S(2)}, u32[]{:S(2)}) collective-permute-start(bf16[1,2,8192]{2,1,0:T(2,128)(2,1)} %bitcast.18), channel_id=1, source_target_pairs={{0,8},{1,9},{2,10},{3,11},{4,12},{5,13},{6,14},{7,15},{8,0},{9,1},... | collective-permute-start | bytes 98312 | tf_op jit(solution)/shard_map/ppermute | solution.py:213
  4.8 1.4 %seed.1 = (s32[13,20]{1,0:T(8,128)S(4)}, s32[69]{0:T(128)S(4)}, s32[69]{0:T(128)S(4)}, s32[1]{0:T(128)S(4)}, bf16[8,2,8192]{2,1,0:T(2,128)(2,1)S(1)}, /*index=5*/bf16[8,2,8192]{2,1,0:T(2,128)(2,1)S(1)}) custom-call(s32[12,20]{1,0:T(8,128)} %rows_ref.1, s32[12]{0:T(128)} %count_ref.1, bf16[2,8192]{1,0:T(2,128)(2,1)} %x_ref.1, bf16[2,8192]{1,0:T(2,128)(2,1)} %dy_ref.1), custom_call_target="tpu_custom_call" | custom-call | tf_op jit(solution)/shard_map/seed/pallas_call | solution.py:252
  6.2 1.0 %collective-permute-done.4 = bf16[1,2,8192]{2,1,0:T(2,128)(2,1)S(1)} collective-permute-done((bf16[1,2,8192]{2,1,0:T(2,128)(2,1)}, bf16[1,2,8192]{2,1,0:T(2,128)(2,1)S(1)}, u32[]{:S(2)}, u32[]{:S(2)}) %collective-permute-start.4) | collective-permute-done | bytes 32800 | tf_op jit(solution)/shard_map/ppermute | solution.py:213
  7.3 1.8 %collective-permute-start.5 = (bf16[2,2,8192]{2,1,0:T(2,128)(2,1)S(1)}, bf16[2,2,8192]{2,1,0:T(2,128)(2,1)S(1)}, u32[]{:S(2)}, u32[]{:S(2)}) collective-permute-start(bf16[2,2,8192]{2,1,0:T(2,128)(2,1)S(1)} %slice.53), channel_id=1, source_target_pairs={{0,2},{1,5},{2,0},{3,7},{4,6},{5,1},{6,4},{7,3},{8,10},{9,13},{10,... | collective-permute-start | bytes 196616 | tf_op jit(solution)/shard_map/ppermute | solution.py:213
  9.1 0.7 %collective-permute-done = bf16[1,2,8192]{2,1,0:T(2,128)(2,1)S(1)} collective-permute-done((bf16[1,2,8192]{2,1,0:T(2,128)(2,1)}, bf16[1,2,8192]{2,1,0:T(2,128)(2,1)S(1)}, u32[]{:S(2)}, u32[]{:S(2)}) %collective-permute-start) | collective-permute-done | bytes 32800 | tf_op jit(solution)/shard_map/ppermute | solution.py:213
  9.8 1.6 %collective-permute-start.1 = (bf16[2,2,8192]{2,1,0:T(2,128)(2,1)S(1)}, bf16[2,2,8192]{2,1,0:T(2,128)(2,1)S(1)}, u32[]{:S(2)}, u32[]{:S(2)}) collective-permute-start(bf16[2,2,8192]{2,1,0:T(2,128)(2,1)S(1)} %slice.51), channel_id=1, source_target_pairs={{0,4},{1,3},{2,6},{3,1},{4,0},{5,7},{6,2},{7,5},{8,12},{9,11},{10,... | collective-permute-start | bytes 196616 | tf_op jit(solution)/shard_map/ppermute | solution.py:213
  11.5 0.6 %collective-permute-done.5 = bf16[2,2,8192]{2,1,0:T(2,128)(2,1)S(1)} collective-permute-done((bf16[2,2,8192]{2,1,0:T(2,128)(2,1)S(1)}, bf16[2,2,8192]{2,1,0:T(2,128)(2,1)S(1)}, u32[]{:S(2)}, u32[]{:S(2)}) %collective-permute-start.5) | collective-permute-done | bytes 65568 | tf_op jit(solution)/shard_map/ppermute | solution.py:213
  12.3 1.8 %collective-permute-start.6 = (bf16[4,2,8192]{2,1,0:T(2,128)(2,1)S(1)}, bf16[4,2,8192]{2,1,0:T(2,128)(2,1)S(1)}, u32[]{:S(2)}, u32[]{:S(2)}) collective-permute-start(bf16[4,2,8192]{2,1,0:T(2,128)(2,1)S(1)} %slice.54), channel_id=1, source_target_pairs={{0,4},{1,3},{2,6},{3,1},{4,0},{5,7},{6,2},{7,5},{8,12},{9,11},{10,... | collective-permute-start | bytes 393224 | tf_op jit(solution)/shard_map/ppermute | solution.py:213
  14.3 1.6 %collective-permute-start.2 = (bf16[4,2,8192]{2,1,0:T(2,128)(2,1)S(1)}, bf16[4,2,8192]{2,1,0:T(2,128)(2,1)S(1)}, u32[]{:S(2)}, u32[]{:S(2)}) collective-permute-start(bf16[4,2,8192]{2,1,0:T(2,128)(2,1)S(1)} %slice.52), channel_id=1, source_target_pairs={{0,2},{1,5},{2,0},{3,7},{4,6},{5,1},{6,4},{7,3},{8,10},{9,13},{10,... | collective-permute-start | bytes 393224 | tf_op jit(solution)/shard_map/ppermute | solution.py:213
  15.9 1.9 %collective-permute-done.6 = bf16[4,2,8192]{2,1,0:T(2,128)(2,1)S(1)} collective-permute-done((bf16[4,2,8192]{2,1,0:T(2,128)(2,1)S(1)}, bf16[4,2,8192]{2,1,0:T(2,128)(2,1)S(1)}, u32[]{:S(2)}, u32[]{:S(2)}) %collective-permute-start.6) | collective-permute-done | bytes 131104 | tf_op jit(solution)/shard_map/ppermute | solution.py:213
  17.9 0.1 constant_dynamic-update-slice_fusion
  18.0 1.3 %collective-permute-done.2 = bf16[4,2,8192]{2,1,0:T(2,128)(2,1)S(1)} collective-permute-done((bf16[4,2,8192]{2,1,0:T(2,128)(2,1)S(1)}, bf16[4,2,8192]{2,1,0:T(2,128)(2,1)S(1)}, u32[]{:S(2)}, u32[]{:S(2)}) %collective-permute-start.2) | collective-permute-done | bytes 131104 | tf_op jit(solution)/shard_map/ppermute | solution.py:213
  19.4 0.1 constant_dynamic-update-slice_fusion.3
  19.6 0.1 reshape.28.x_near
  19.7 0.2 copy.21
  19.9 0.1 reshape.31.dy_near
  20.0 0.2 copy.20
  20.2 0.1 reshape.33.dy_far
  20.3 0.8 %collective-permute-done.3 = bf16[8,2,8192]{2,1,0:T(2,128)(2,1)S(1)} collective-permute-done((bf16[8,2,8192]{2,1,0:T(2,128)(2,1)S(1)}, bf16[8,2,8192]{2,1,0:T(2,128)(2,1)S(1)}, u32[]{:S(2)}, u32[]{:S(2)}) %collective-permute-start.3) | collective-permute-done | bytes 262176 | tf_op jit(solution)/shard_map/ppermute | solution.py:213
  21.1 0.1 reshape.29.x_far
  21.2 12.5 %layer.1 = (bf16[13,32,128]{2,1,0:T(8,128)(2,1)S(1)}, bf16[13,32,256]{2,1,0:T(8,128)(2,1)S(1)}, bf16[65,32,128]{2,1,0:T(8,128)(2,1)S(1)}, bf16[65,32,128]{2,1,0:...) custom-call(s32[13,20]{1,0:T(8,128)S(4)} %get-tuple-element.31.live_ref.refs_0_, ...), custom_call_target="tpu_custom_call" | custom-call | flops 1509949440 | bytes 23592960 | tf_op jit(solution)/shard_map/layer/pallas_call | solution.py:275
  33.7 2.8 %gate_up_grad.3 = (bf16[12,20,128,128]{3,2,1,0:T(8,128)(2,1)}, bf16[12,20,128,128]{3,2,1,0:T(8,128)(2,1)}) custom-call(s32[13,20]{1,0:T(8,128)S(4)} %get-tuple-element.31.live_ref.refs_0_, bf16[65,32,128]{2,1,0:T(8,128)(2,1)S(1)} %get-tuple-element.39.refs_1_, bf16[13,32,256]{2,1,0:T(8,128)(2,1)S(1)} %get-tuple-element.40.refs_2_), custom_call_target="tpu_custom_call" | custom-call | flops 167772160 | bytes 5242880 | tf_op jit(solution)/shard_map/gate_up_grad/pallas_call | solution.py:299
  36.7 1.7 %collective-permute-start.9 = (bf16[2,8,8192]{2,1,0:T(8,128)(2,1)S(1)}, bf16[2,8,8192]{2,1,0:T(8,128)(2,1)S(1)}, u32[]{:S(2)}, u32[]{:S(2)}) collective-permute-start(bf16[2,8,8192]{2,1,0:T(8,128)(2,1)S(1)} %slice.73.refs_3_), channel_id=1, source_target_pairs={{0,2},{1,5},{2,0},{3,7},{4,6},{5,1},{6,4},{7,3},{8,10},{9,13},{10,... | collective-permute-start | bytes 786440 | tf_op jit(solution)/shard_map/ppermute | solution.py:213
  38.4 3.6 %down_grad.1 = bf16[12,20,128,128]{3,2,1,0:T(8,128)(2,1)} custom-call(s32[13,20]{1,0:T(8,128)S(4)} %get-tuple-element.31.live_ref.refs_0_, bf16[65,32,128]{2,1,0:T(8,128)(2,1)S(1)} %get-tuple-element.44.refs_1_, bf16[13,32,128]{2,1,0:T(8,128)(2,1)S(1)} %get-tuple-element.45.refs_2_, bf16[2,8,8192]{2,1,0:T(8,128)(2,1)S(1)} %slice.73.refs_3_), custom_call_target="tpu_custom_call" | custom-call | flops 251658240 | bytes 7864320 | tf_op jit(solution)/shard_map/down_grad/pallas_call | solution.py:299
  42.1 1.1 %collective-permute-done.9 = bf16[2,8,8192]{2,1,0:T(8,128)(2,1)S(1)} collective-permute-done((bf16[2,8,8192]{2,1,0:T(8,128)(2,1)S(1)}, bf16[2,8,8192]{2,1,0:T(8,128)(2,1)S(1)}, u32[]{:S(2)}, u32[]{:S(2)}) %collective-permute-start.9) | collective-permute-done | bytes 262176 | tf_op jit(solution)/shard_map/ppermute | solution.py:213
  43.3 1.0 %collective-permute-start.10 = (bf16[2,4,8192]{2,1,0:T(4,128)(2,1)S(1)}, bf16[2,4,8192]{2,1,0:T(4,128)(2,1)S(1)}, u32[]{:S(2)}, u32[]{:S(2)}) collective-permute-start(bf16[2,4,8192]{2,1,0:T(4,128)(2,1)S(1)} %slice.74.refs_5_), channel_id=1, source_target_pairs={{0,4},{1,3},{2,6},{3,1},{4,0},{5,7},{6,2},{7,5},{8,12},{9,11},{10,... | collective-permute-start | bytes 393224 | tf_op jit(solution)/shard_map/ppermute | solution.py:213
  44.2 2.8 %gate_up_grad.4 = (bf16[12,20,128,128]{3,2,1,0:T(8,128)(2,1)}, bf16[12,20,128,128]{3,2,1,0:T(8,128)(2,1)}) custom-call(s32[13,20]{1,0:T(8,128)S(4)} %get-tuple-element.31.live_ref.refs_0_, bf16[65,32,128]{2,1,0:T(8,128)(2,1)S(1)} %get-tuple-element.39.refs_1_, ...), custom_call_target="tpu_custom_call", output_to_operand_aliasing={{0}: (3, {}), {1}: (4, {})} | custom-call | flops 167772160 | bytes 5242880 | tf_op jit(solution)/shard_map/gate_up_grad/pallas_call | solution.py:299
  47.1 1.2 %collective-permute-done.10 = bf16[2,4,8192]{2,1,0:T(4,128)(2,1)S(1)} collective-permute-done((bf16[2,4,8192]{2,1,0:T(4,128)(2,1)S(1)}, bf16[2,4,8192]{2,1,0:T(4,128)(2,1)S(1)}, u32[]{:S(2)}, u32[]{:S(2)}) %collective-permute-start.10) | collective-permute-done | bytes 131104 | tf_op jit(solution)/shard_map/ppermute | solution.py:213
  48.4 3.1 %collective-permute-start.11 = (bf16[2,2,8192]{2,1,0:T(2,128)(2,1)S(1)}, bf16[2,2,8192]{2,1,0:T(2,128)(2,1)S(1)}, u32[]{:S(2)}, u32[]{:S(2)}) collective-permute-start(bf16[2,2,8192]{2,1,0:T(2,128)(2,1)S(1)} %slice.75.refs_5_), channel_id=1, source_target_pairs={{0,8},{1,9},{2,10},{3,11},{4,12},{5,13},{6,14},{7,15},{8,0},{9,1},... | collective-permute-start | bytes 196616 | tf_op jit(solution)/shard_map/ppermute | solution.py:213
  51.5 2.8 %gate_up_grad.5 = (bf16[12,20,128,128]{3,2,1,0:T(8,128)(2,1)}, bf16[12,20,128,128]{3,2,1,0:T(8,128)(2,1)}) custom-call(s32[13,20]{1,0:T(8,128)S(4)} %get-tuple-element.31.live_ref.refs_0_, bf16[65,32,128]{2,1,0:T(8,128)(2,1)S(1)} %get-tuple-element.39.refs_1_, ...), custom_call_target="tpu_custom_call", output_to_operand_aliasing={{0}: (3, {}), {1}: (4, {})} | custom-call | flops 167772160 | bytes 5242880 | tf_op jit(solution)/shard_map/gate_up_grad/pallas_call | solution.py:299
  54.3 0.1 collective-permute-done.11
  54.5 0.7 %slice_bitcast_fusion = (bf16[2,8192]{1,0:T(2,128)(2,1)}, bf16[2,8192]{1,0:T(2,128)(2,1)}) fusion(bf16[2,2,8192]{2,1,0:T(2,128)(2,1)S(1)} %fusion), kind=kLoop, calls=%fused_computation.10 | loop fusion | bytes 131072 | tf_op jit(solution)/shard_map/squeeze | solution.py:342
  (22 shorter events, 1.2 us)
Async XLA Ops:
  0.6 6.6 %collective-permute-start.4 = (bf16[1,2,8192]{2,1,0:T(2,128)(2,1)}, bf16[1,2,8192]{2,1,0:T(2,128)(2,1)S(1)}, u32[]{:S(2)}, u32[]{:S(2)}) collective-permute-start(bf16[1,2,8192]{2,1,0:T(2,128)(2,1)} %bitcast.18), channel_id=1, source_target_pairs={{0,8},{1,9},{2,10},{3,11},{4,12},{5,13},{6,14},{7,15},{8,0},{9,1},... | collective-permute-start | bytes 98312 | tf_op jit(solution)/shard_map/ppermute | solution.py:213
  4.7 5.0 %collective-permute-start = (bf16[1,2,8192]{2,1,0:T(2,128)(2,1)}, bf16[1,2,8192]{2,1,0:T(2,128)(2,1)S(1)}, u32[]{:S(2)}, u32[]{:S(2)}) collective-permute-start(bf16[1,2,8192]{2,1,0:T(2,128)(2,1)} %bitcast.19), channel_id=1, source_target_pairs={{0,8},{1,9},{2,10},{3,11},{4,12},{5,13},{6,14},{7,15},{8,0},{9,1},... | collective-permute-start | bytes 98312 | tf_op jit(solution)/shard_map/ppermute | solution.py:213
  7.3 4.8 %collective-permute-start.5 = (bf16[2,2,8192]{2,1,0:T(2,128)(2,1)S(1)}, bf16[2,2,8192]{2,1,0:T(2,128)(2,1)S(1)}, u32[]{:S(2)}, u32[]{:S(2)}) collective-permute-start(bf16[2,2,8192]{2,1,0:T(2,128)(2,1)S(1)} %slice.53), channel_id=1, source_target_pairs={{0,2},{1,5},{2,0},{3,7},{4,6},{5,1},{6,4},{7,3},{8,10},{9,13},{10,... | collective-permute-start | bytes 196616 | tf_op jit(solution)/shard_map/ppermute | solution.py:213
  9.8 4.3 %collective-permute-start.1 = (bf16[2,2,8192]{2,1,0:T(2,128)(2,1)S(1)}, bf16[2,2,8192]{2,1,0:T(2,128)(2,1)S(1)}, u32[]{:S(2)}, u32[]{:S(2)}) collective-permute-start(bf16[2,2,8192]{2,1,0:T(2,128)(2,1)S(1)} %slice.51), channel_id=1, source_target_pairs={{0,4},{1,3},{2,6},{3,1},{4,0},{5,7},{6,2},{7,5},{8,12},{9,11},{10,... | collective-permute-start | bytes 196616 | tf_op jit(solution)/shard_map/ppermute | solution.py:213
  12.3 5.6 %collective-permute-start.6 = (bf16[4,2,8192]{2,1,0:T(2,128)(2,1)S(1)}, bf16[4,2,8192]{2,1,0:T(2,128)(2,1)S(1)}, u32[]{:S(2)}, u32[]{:S(2)}) collective-permute-start(bf16[4,2,8192]{2,1,0:T(2,128)(2,1)S(1)} %slice.54), channel_id=1, source_target_pairs={{0,4},{1,3},{2,6},{3,1},{4,0},{5,7},{6,2},{7,5},{8,12},{9,11},{10,... | collective-permute-start | bytes 393224 | tf_op jit(solution)/shard_map/ppermute | solution.py:213
  14.3 5.0 %collective-permute-start.2 = (bf16[4,2,8192]{2,1,0:T(2,128)(2,1)S(1)}, bf16[4,2,8192]{2,1,0:T(2,128)(2,1)S(1)}, u32[]{:S(2)}, u32[]{:S(2)}) collective-permute-start(bf16[4,2,8192]{2,1,0:T(2,128)(2,1)S(1)} %slice.52), channel_id=1, source_target_pairs={{0,2},{1,5},{2,0},{3,7},{4,6},{5,1},{6,4},{7,3},{8,10},{9,13},{10,... | collective-permute-start | bytes 393224 | tf_op jit(solution)/shard_map/ppermute | solution.py:213
  18.0 2.0 %collective-permute-start.7 = (bf16[8,2,8192]{2,1,0:T(2,128)(2,1)S(1)}, bf16[8,2,8192]{2,1,0:T(2,128)(2,1)S(1)}, u32[]{:S(2)}, u32[]{:S(2)}) collective-permute-start(bf16[8,2,8192]{2,1,0:T(2,128)(2,1)S(1)} %constant_dynamic-update-slice_fusion), channel_id=1, source_target_pairs={{0,1},{1,0},{2,3},{3,2},{4,5},{5,4},{6,7},{7,6},{8,9},{9,8},{10,11... | collective-permute-start | bytes 786440 | tf_op jit(solution)/shard_map/ppermute | solution.py:213
  19.5 1.6 %collective-permute-start.3 = (bf16[8,2,8192]{2,1,0:T(2,128)(2,1)S(1)}, bf16[8,2,8192]{2,1,0:T(2,128)(2,1)S(1)}, u32[]{:S(2)}, u32[]{:S(2)}) collective-permute-start(bf16[8,2,8192]{2,1,0:T(2,128)(2,1)S(1)} %constant_dynamic-update-slice_fusion.3), channel_id=1, source_target_pairs={{0,1},{1,0},{2,3},{3,2},{4,5},{5,4},{6,7},{7,6},{8,9},{9,8},{10,11... | collective-permute-start | bytes 786440 | tf_op jit(solution)/shard_map/ppermute | solution.py:213
  33.7 2.9 %collective-permute-start.8 = (bf16[2,16,8192]{2,1,0:T(8,128)(2,1)S(1)}, bf16[2,16,8192]{2,1,0:T(8,128)(2,1)S(1)}, u32[]{:S(2)}, u32[]{:S(2)}) collective-permute-start(bf16[2,16,8192]{2,1,0:T(8,128)(2,1)S(1)} %get-tuple-element.38), channel_id=1, source_target_pairs={{0,1},{1,0},{2,3},{3,2},{4,5},{5,4},{6,7},{7,6},{8,9},{9,8},{10,11... | collective-permute-start | bytes 1572872 | tf_op jit(solution)/shard_map/ppermute | solution.py:213
  36.7 6.4 %collective-permute-start.9 = (bf16[2,8,8192]{2,1,0:T(8,128)(2,1)S(1)}, bf16[2,8,8192]{2,1,0:T(8,128)(2,1)S(1)}, u32[]{:S(2)}, u32[]{:S(2)}) collective-permute-start(bf16[2,8,8192]{2,1,0:T(8,128)(2,1)S(1)} %slice.73.refs_3_), channel_id=1, source_target_pairs={{0,2},{1,5},{2,0},{3,7},{4,6},{5,1},{6,4},{7,3},{8,10},{9,13},{10,... | collective-permute-start | bytes 786440 | tf_op jit(solution)/shard_map/ppermute | solution.py:213
  43.3 5.0 %collective-permute-start.10 = (bf16[2,4,8192]{2,1,0:T(4,128)(2,1)S(1)}, bf16[2,4,8192]{2,1,0:T(4,128)(2,1)S(1)}, u32[]{:S(2)}, u32[]{:S(2)}) collective-permute-start(bf16[2,4,8192]{2,1,0:T(4,128)(2,1)S(1)} %slice.74.refs_5_), channel_id=1, source_target_pairs={{0,4},{1,3},{2,6},{3,1},{4,0},{5,7},{6,2},{7,5},{8,12},{9,11},{10,... | collective-permute-start | bytes 393224 | tf_op jit(solution)/shard_map/ppermute | solution.py:213
  48.4 6.0 %collective-permute-start.11 = (bf16[2,2,8192]{2,1,0:T(2,128)(2,1)S(1)}, bf16[2,2,8192]{2,1,0:T(2,128)(2,1)S(1)}, u32[]{:S(2)}, u32[]{:S(2)}) collective-permute-start(bf16[2,2,8192]{2,1,0:T(2,128)(2,1)S(1)} %slice.75.refs_5_), channel_id=1, source_target_pairs={{0,8},{1,9},{2,10},{3,11},{4,12},{5,13},{6,14},{7,15},{8,0},{9,1},... | collective-permute-start | bytes 196616 | tf_op jit(solution)/shard_map/ppermute | solution.py:213

commit v2 on v1

--- a/solution.py
+++ b/solution.py
@@ -7,7 +7,6 @@
 from jax.experimental.pallas import tpu as pltpu
 from jax.sharding import PartitionSpec as P
 
-NT = (((1,), (1,)), ((), ()))
 TN = (((0,), (0,)), ((), ()))
 CHUNK = 4
 STEP = 4
@@ -98,9 +97,8 @@
         xg = jnp.concatenate([xpad_ref[r] for r in rows], axis=1)
         dyg = jnp.concatenate([dypad_ref[r] for r in rows], axis=1)
         pre = jnp.dot(xg, gate_up_tiles(tiles, s), preferred_element_type=jnp.float32)
-        d_hidden = lax.dot_general(
-            dyg, down_tiles(tiles, s), NT, preferred_element_type=jnp.float32
-        )
+        turned = jnp.dot(down_tiles(tiles, s), dyg.T, preferred_element_type=jnp.float32)
+        d_hidden = turned.T
         pre_acc[c, :, : 2 * blk] += pre
         pre_acc[c, :, 2 * blk :] += d_hidden
 
@@ -185,7 +183,7 @@
             for k, (stage, grad) in enumerate(zip(stages, grad_refs))
         ]
 
-    group = max(k for k in range(1, 5) if count % k == 0)
+    group = max(k for k in range(1, 6) if count % k == 0)
 
     def step(g, carry):
         some = [g * group + k for k in range(group)]
@@ -311,8 +309,9 @@
             name=name,
         )(live, pad, factor, *earlier, *after)
 
-    third = -(-blocks // 3)
-    cuts = {0: (0, third), 2: (third, 2 * third), 3: (2 * third, blocks)}
+    near = max(1, blocks // 6)
+    middle = near + (blocks - near + 1) // 2
+    cuts = {0: (0, near), 2: (near, middle), 3: (middle, blocks)}
     gate_up, down_grad, after = [], None, []
     for i, bits in enumerate([cores] + x_hops[::-1]):
         got = swap(send, bits, n)

time: 55.8 us -> 54.1 us (0.970)
  waiting for transfers between devices: 8.83 us -> 7.34 us
    ppermute x12, waiting for transfers between devices: 8.83 us -> 7.34 us  [swap(): return lax.ppermute(value, 'col', [(j, j ^ bits[j % 2]) for j in range(n)])]
  transfers between devices with their start and end apart: 12 -> 12, of which waited for: 10 -> 9; matrix products, arithmetic and copies ran while one was open for 2% -> 3% of each run, Pallas kernels for 25% -> 25%
where the time goes in v2:
time: 54.1 us; the launch traced here: 53.6 us
  Pallas kernels  25.5 us (47%)
  starting transfers between devices  17.4 us (32%)
  waiting for transfers between devices  7.34 us (14%)
  local copies, waits for them, and re-layouts  2.28 us (4%)
  between operations  0.85 us (2%)
    ppermute x12, starting transfers between devices, swap(): return lax.ppermute(value, 'col', [(j, j ^ bits[j % 2]) for j in range(n)])  17.4 us
    pallas_call x4, Pallas kernels, grads(): pl.pallas_call(functools.partial(grad_kernel, products, first, count, out...  12.1 us
    pallas_call x1, Pallas kernels, local(): pl.pallas_call(layer_kernel, in_specs=[smem] * 4 + [vmem] * 4 + [hbm] * 3...  12.1 us
    ppermute x12, waiting for transfers between devices, swap(): return lax.ppermute(value, 'col', [(j, j ^ bits[j % 2]) for j in range(n)])  7.34 us
    pallas_call x1, Pallas kernels, local(): pl.pallas_call(functools.partial(seed_kernel, width // blk), in_specs=[sm...  1.41 us
  transfers between devices with their start and end apart: 12, of which 9 were waited for; matrix products, arithmetic and copies ran while one was open for 3% of the time, Pallas kernels for 25%

profile of v2, /device:TPU:0, one launch (start us, length us, event | category | flops | bytes accessed | tf_op | source)
XLA Modules:
  0.0 53.6 jit_solution(15318538457455526921)
XLA Ops:
  0.6 4.1 %collective-permute-start.4 = (bf16[1,2,8192]{2,1,0:T(2,128)(2,1)}, bf16[1,2,8192]{2,1,0:T(2,128)(2,1)S(1)}, u32[]{:S(2)}, u32[]{:S(2)}) collective-permute-start(bf16[1,2,8192]{2,1,0:T(2,128)(2,1)} %bitcast.18), channel_id=1, source_target_pairs={{0,8},{1,9},{2,10},{3,11},{4,12},{5,13},{6,14},{7,15},{8,0},{9,1},... | collective-permute-start | bytes 98312 | tf_op jit(solution)/shard_map/ppermute | solution.py:211
  4.8 1.4 %seed.1 = (s32[13,20]{1,0:T(8,128)S(4)}, s32[69]{0:T(128)S(4)}, s32[69]{0:T(128)S(4)}, s32[1]{0:T(128)S(4)}, bf16[8,2,8192]{2,1,0:T(2,128)(2,1)S(1)}, /*index=5*/bf16[8,2,8192]{2,1,0:T(2,128)(2,1)S(1)}) custom-call(s32[12,20]{1,0:T(8,128)} %rows_ref.1, s32[12]{0:T(128)} %count_ref.1, bf16[2,8192]{1,0:T(2,128)(2,1)} %x_ref.1, bf16[2,8192]{1,0:T(2,128)(2,1)} %dy_ref.1), custom_call_target="tpu_custom_call" | custom-call | tf_op jit(solution)/shard_map/seed/pallas_call | solution.py:250
  6.2 1.0 %collective-permute-done.4 = bf16[1,2,8192]{2,1,0:T(2,128)(2,1)S(1)} collective-permute-done((bf16[1,2,8192]{2,1,0:T(2,128)(2,1)}, bf16[1,2,8192]{2,1,0:T(2,128)(2,1)S(1)}, u32[]{:S(2)}, u32[]{:S(2)}) %collective-permute-start.4) | collective-permute-done | bytes 32800 | tf_op jit(solution)/shard_map/ppermute | solution.py:211
  7.3 1.8 %collective-permute-start.5 = (bf16[2,2,8192]{2,1,0:T(2,128)(2,1)S(1)}, bf16[2,2,8192]{2,1,0:T(2,128)(2,1)S(1)}, u32[]{:S(2)}, u32[]{:S(2)}) collective-permute-start(bf16[2,2,8192]{2,1,0:T(2,128)(2,1)S(1)} %slice.53), channel_id=1, source_target_pairs={{0,2},{1,5},{2,0},{3,7},{4,6},{5,1},{6,4},{7,3},{8,10},{9,13},{10,... | collective-permute-start | bytes 196616 | tf_op jit(solution)/shard_map/ppermute | solution.py:211
  9.1 0.7 %collective-permute-done = bf16[1,2,8192]{2,1,0:T(2,128)(2,1)S(1)} collective-permute-done((bf16[1,2,8192]{2,1,0:T(2,128)(2,1)}, bf16[1,2,8192]{2,1,0:T(2,128)(2,1)S(1)}, u32[]{:S(2)}, u32[]{:S(2)}) %collective-permute-start) | collective-permute-done | bytes 32800 | tf_op jit(solution)/shard_map/ppermute | solution.py:211
  9.8 1.6 %collective-permute-start.1 = (bf16[2,2,8192]{2,1,0:T(2,128)(2,1)S(1)}, bf16[2,2,8192]{2,1,0:T(2,128)(2,1)S(1)}, u32[]{:S(2)}, u32[]{:S(2)}) collective-permute-start(bf16[2,2,8192]{2,1,0:T(2,128)(2,1)S(1)} %slice.51), channel_id=1, source_target_pairs={{0,4},{1,3},{2,6},{3,1},{4,0},{5,7},{6,2},{7,5},{8,12},{9,11},{10,... | collective-permute-start | bytes 196616 | tf_op jit(solution)/shard_map/ppermute | solution.py:211
  11.5 0.6 %collective-permute-done.5 = bf16[2,2,8192]{2,1,0:T(2,128)(2,1)S(1)} collective-permute-done((bf16[2,2,8192]{2,1,0:T(2,128)(2,1)S(1)}, bf16[2,2,8192]{2,1,0:T(2,128)(2,1)S(1)}, u32[]{:S(2)}, u32[]{:S(2)}) %collective-permute-start.5) | collective-permute-done | bytes 65568 | tf_op jit(solution)/shard_map/ppermute | solution.py:211
  12.3 1.8 %collective-permute-start.6 = (bf16[4,2,8192]{2,1,0:T(2,128)(2,1)S(1)}, bf16[4,2,8192]{2,1,0:T(2,128)(2,1)S(1)}, u32[]{:S(2)}, u32[]{:S(2)}) collective-permute-start(bf16[4,2,8192]{2,1,0:T(2,128)(2,1)S(1)} %slice.54), channel_id=1, source_target_pairs={{0,4},{1,3},{2,6},{3,1},{4,0},{5,7},{6,2},{7,5},{8,12},{9,11},{10,... | collective-permute-start | bytes 393224 | tf_op jit(solution)/shard_map/ppermute | solution.py:211
  14.3 1.6 %collective-permute-start.2 = (bf16[4,2,8192]{2,1,0:T(2,128)(2,1)S(1)}, bf16[4,2,8192]{2,1,0:T(2,128)(2,1)S(1)}, u32[]{:S(2)}, u32[]{:S(2)}) collective-permute-start(bf16[4,2,8192]{2,1,0:T(2,128)(2,1)S(1)} %slice.52), channel_id=1, source_target_pairs={{0,2},{1,5},{2,0},{3,7},{4,6},{5,1},{6,4},{7,3},{8,10},{9,13},{10,... | collective-permute-start | bytes 393224 | tf_op jit(solution)/shard_map/ppermute | solution.py:211
  15.9 1.9 %collective-permute-done.6 = bf16[4,2,8192]{2,1,0:T(2,128)(2,1)S(1)} collective-permute-done((bf16[4,2,8192]{2,1,0:T(2,128)(2,1)S(1)}, bf16[4,2,8192]{2,1,0:T(2,128)(2,1)S(1)}, u32[]{:S(2)}, u32[]{:S(2)}) %collective-permute-start.6) | collective-permute-done | bytes 131104 | tf_op jit(solution)/shard_map/ppermute | solution.py:211
  17.9 0.1 constant_dynamic-update-slice_fusion
  18.0 1.3 %collective-permute-done.2 = bf16[4,2,8192]{2,1,0:T(2,128)(2,1)S(1)} collective-permute-done((bf16[4,2,8192]{2,1,0:T(2,128)(2,1)S(1)}, bf16[4,2,8192]{2,1,0:T(2,128)(2,1)S(1)}, u32[]{:S(2)}, u32[]{:S(2)}) %collective-permute-start.2) | collective-permute-done | bytes 131104 | tf_op jit(solution)/shard_map/ppermute | solution.py:211
  19.4 0.1 constant_dynamic-update-slice_fusion.3
  19.6 0.1 reshape.28.x_near
  19.7 0.2 copy.21
  19.9 0.1 reshape.31.dy_near
  20.0 0.2 copy.20
  20.2 0.1 reshape.33.dy_far
  20.3 0.8 %collective-permute-done.3 = bf16[8,2,8192]{2,1,0:T(2,128)(2,1)S(1)} collective-permute-done((bf16[8,2,8192]{2,1,0:T(2,128)(2,1)S(1)}, bf16[8,2,8192]{2,1,0:T(2,128)(2,1)S(1)}, u32[]{:S(2)}, u32[]{:S(2)}) %collective-permute-start.3) | collective-permute-done | bytes 262176 | tf_op jit(solution)/shard_map/ppermute | solution.py:211
  21.1 0.1 reshape.29.x_far
  21.2 12.1 %layer.1 = (bf16[13,32,128]{2,1,0:T(8,128)(2,1)S(1)}, bf16[13,32,256]{2,1,0:T(8,128)(2,1)S(1)}, bf16[65,32,128]{2,1,0:T(8,128)(2,1)S(1)}, bf16[65,32,128]{2,1,0:...) custom-call(s32[13,20]{1,0:T(8,128)S(4)} %get-tuple-element.31.live_ref.refs_0_, ...), custom_call_target="tpu_custom_call" | custom-call | flops 1509949440 | bytes 23592960 | tf_op jit(solution)/shard_map/layer/pallas_call | solution.py:273
  33.2 0.4 collective-permute-start.8
  33.6 1.9 %gate_up_grad.3 = (bf16[12,20,128,128]{3,2,1,0:T(8,128)(2,1)}, bf16[12,20,128,128]{3,2,1,0:T(8,128)(2,1)}) custom-call(s32[13,20]{1,0:T(8,128)S(4)} %get-tuple-element.31.live_ref.refs_0_, bf16[65,32,128]{2,1,0:T(8,128)(2,1)S(1)} %get-tuple-element.39.refs_1_, bf16[13,32,256]{2,1,0:T(8,128)(2,1)S(1)} %get-tuple-element.40.refs_2_), custom_call_target="tpu_custom_call" | custom-call | flops 83886080 | bytes 2621440 | tf_op jit(solution)/shard_map/gate_up_grad/pallas_call | solution.py:297
  35.7 2.0 %collective-permute-start.9 = (bf16[2,8,8192]{2,1,0:T(8,128)(2,1)S(1)}, bf16[2,8,8192]{2,1,0:T(8,128)(2,1)S(1)}, u32[]{:S(2)}, u32[]{:S(2)}) collective-permute-start(bf16[2,8,8192]{2,1,0:T(8,128)(2,1)S(1)} %slice.73.refs_3_), channel_id=1, source_target_pairs={{0,2},{1,5},{2,0},{3,7},{4,6},{5,1},{6,4},{7,3},{8,10},{9,13},{10,... | collective-permute-start | bytes 786440 | tf_op jit(solution)/shard_map/ppermute | solution.py:211
  37.7 3.6 %down_grad.1 = bf16[12,20,128,128]{3,2,1,0:T(8,128)(2,1)} custom-call(s32[13,20]{1,0:T(8,128)S(4)} %get-tuple-element.31.live_ref.refs_0_, bf16[65,32,128]{2,1,0:T(8,128)(2,1)S(1)} %get-tuple-element.44.refs_1_, bf16[13,32,128]{2,1,0:T(8,128)(2,1)S(1)} %get-tuple-element.45.refs_2_, bf16[2,8,8192]{2,1,0:T(8,128)(2,1)S(1)} %slice.73.refs_3_), custom_call_target="tpu_custom_call" | custom-call | flops 251658240 | bytes 7864320 | tf_op jit(solution)/shard_map/down_grad/pallas_call | solution.py:297
  41.3 0.8 %collective-permute-done.9 = bf16[2,8,8192]{2,1,0:T(8,128)(2,1)S(1)} collective-permute-done((bf16[2,8,8192]{2,1,0:T(8,128)(2,1)S(1)}, bf16[2,8,8192]{2,1,0:T(8,128)(2,1)S(1)}, u32[]{:S(2)}, u32[]{:S(2)}) %collective-permute-start.9) | collective-permute-done | bytes 262176 | tf_op jit(solution)/shard_map/ppermute | solution.py:211
  42.2 2.0 %collective-permute-start.10 = (bf16[2,4,8192]{2,1,0:T(4,128)(2,1)S(1)}, bf16[2,4,8192]{2,1,0:T(4,128)(2,1)S(1)}, u32[]{:S(2)}, u32[]{:S(2)}) collective-permute-start(bf16[2,4,8192]{2,1,0:T(4,128)(2,1)S(1)} %slice.74.refs_5_), channel_id=1, source_target_pairs={{0,4},{1,3},{2,6},{3,1},{4,0},{5,7},{6,2},{7,5},{8,12},{9,11},{10,... | collective-permute-start | bytes 393224 | tf_op jit(solution)/shard_map/ppermute | solution.py:211
  44.2 3.3 %gate_up_grad.4 = (bf16[12,20,128,128]{3,2,1,0:T(8,128)(2,1)}, bf16[12,20,128,128]{3,2,1,0:T(8,128)(2,1)}) custom-call(s32[13,20]{1,0:T(8,128)S(4)} %get-tuple-element.31.live_ref.refs_0_, bf16[65,32,128]{2,1,0:T(8,128)(2,1)S(1)} %get-tuple-element.39.refs_1_, ...), custom_call_target="tpu_custom_call", output_to_operand_aliasing={{0}: (3, {}), {1}: (4, {})} | custom-call | flops 209715200 | bytes 6553600 | tf_op jit(solution)/shard_map/gate_up_grad/pallas_call | solution.py:297
  47.7 1.8 %collective-permute-start.11 = (bf16[2,2,8192]{2,1,0:T(2,128)(2,1)S(1)}, bf16[2,2,8192]{2,1,0:T(2,128)(2,1)S(1)}, u32[]{:S(2)}, u32[]{:S(2)}) collective-permute-start(bf16[2,2,8192]{2,1,0:T(2,128)(2,1)S(1)} %slice.75.refs_5_), channel_id=1, source_target_pairs={{0,8},{1,9},{2,10},{3,11},{4,12},{5,13},{6,14},{7,15},{8,0},{9,1},... | collective-permute-start | bytes 196616 | tf_op jit(solution)/shard_map/ppermute | solution.py:211
  49.5 3.3 %gate_up_grad.5 = (bf16[12,20,128,128]{3,2,1,0:T(8,128)(2,1)}, bf16[12,20,128,128]{3,2,1,0:T(8,128)(2,1)}) custom-call(s32[13,20]{1,0:T(8,128)S(4)} %get-tuple-element.31.live_ref.refs_0_, bf16[65,32,128]{2,1,0:T(8,128)(2,1)S(1)} %get-tuple-element.39.refs_1_, ...), custom_call_target="tpu_custom_call", output_to_operand_aliasing={{0}: (3, {}), {1}: (4, {})} | custom-call | flops 209715200 | bytes 6553600 | tf_op jit(solution)/shard_map/gate_up_grad/pallas_call | solution.py:297
  52.7 0.1 collective-permute-done.11
  53.0 0.7 %slice_bitcast_fusion = (bf16[2,8192]{1,0:T(2,128)(2,1)}, bf16[2,8192]{1,0:T(2,128)(2,1)}) fusion(bf16[2,2,8192]{2,1,0:T(2,128)(2,1)S(1)} %fusion), kind=kLoop, calls=%fused_computation.10 | loop fusion | bytes 131072 | tf_op jit(solution)/shard_map/squeeze | solution.py:341
  (22 shorter events, 1.2 us)
Async XLA Ops:
  0.6 6.6 %collective-permute-start.4 = (bf16[1,2,8192]{2,1,0:T(2,128)(2,1)}, bf16[1,2,8192]{2,1,0:T(2,128)(2,1)S(1)}, u32[]{:S(2)}, u32[]{:S(2)}) collective-permute-start(bf16[1,2,8192]{2,1,0:T(2,128)(2,1)} %bitcast.18), channel_id=1, source_target_pairs={{0,8},{1,9},{2,10},{3,11},{4,12},{5,13},{6,14},{7,15},{8,0},{9,1},... | collective-permute-start | bytes 98312 | tf_op jit(solution)/shard_map/ppermute | solution.py:211
  4.7 5.0 %collective-permute-start = (bf16[1,2,8192]{2,1,0:T(2,128)(2,1)}, bf16[1,2,8192]{2,1,0:T(2,128)(2,1)S(1)}, u32[]{:S(2)}, u32[]{:S(2)}) collective-permute-start(bf16[1,2,8192]{2,1,0:T(2,128)(2,1)} %bitcast.19), channel_id=1, source_target_pairs={{0,8},{1,9},{2,10},{3,11},{4,12},{5,13},{6,14},{7,15},{8,0},{9,1},... | collective-permute-start | bytes 98312 | tf_op jit(solution)/shard_map/ppermute | solution.py:211
  7.3 4.8 %collective-permute-start.5 = (bf16[2,2,8192]{2,1,0:T(2,128)(2,1)S(1)}, bf16[2,2,8192]{2,1,0:T(2,128)(2,1)S(1)}, u32[]{:S(2)}, u32[]{:S(2)}) collective-permute-start(bf16[2,2,8192]{2,1,0:T(2,128)(2,1)S(1)} %slice.53), channel_id=1, source_target_pairs={{0,2},{1,5},{2,0},{3,7},{4,6},{5,1},{6,4},{7,3},{8,10},{9,13},{10,... | collective-permute-start | bytes 196616 | tf_op jit(solution)/shard_map/ppermute | solution.py:211
  9.8 4.3 %collective-permute-start.1 = (bf16[2,2,8192]{2,1,0:T(2,128)(2,1)S(1)}, bf16[2,2,8192]{2,1,0:T(2,128)(2,1)S(1)}, u32[]{:S(2)}, u32[]{:S(2)}) collective-permute-start(bf16[2,2,8192]{2,1,0:T(2,128)(2,1)S(1)} %slice.51), channel_id=1, source_target_pairs={{0,4},{1,3},{2,6},{3,1},{4,0},{5,7},{6,2},{7,5},{8,12},{9,11},{10,... | collective-permute-start | bytes 196616 | tf_op jit(solution)/shard_map/ppermute | solution.py:211
  12.3 5.6 %collective-permute-start.6 = (bf16[4,2,8192]{2,1,0:T(2,128)(2,1)S(1)}, bf16[4,2,8192]{2,1,0:T(2,128)(2,1)S(1)}, u32[]{:S(2)}, u32[]{:S(2)}) collective-permute-start(bf16[4,2,8192]{2,1,0:T(2,128)(2,1)S(1)} %slice.54), channel_id=1, source_target_pairs={{0,4},{1,3},{2,6},{3,1},{4,0},{5,7},{6,2},{7,5},{8,12},{9,11},{10,... | collective-permute-start | bytes 393224 | tf_op jit(solution)/shard_map/ppermute | solution.py:211
  14.3 5.0 %collective-permute-start.2 = (bf16[4,2,8192]{2,1,0:T(2,128)(2,1)S(1)}, bf16[4,2,8192]{2,1,0:T(2,128)(2,1)S(1)}, u32[]{:S(2)}, u32[]{:S(2)}) collective-permute-start(bf16[4,2,8192]{2,1,0:T(2,128)(2,1)S(1)} %slice.52), channel_id=1, source_target_pairs={{0,2},{1,5},{2,0},{3,7},{4,6},{5,1},{6,4},{7,3},{8,10},{9,13},{10,... | collective-permute-start | bytes 393224 | tf_op jit(solution)/shard_map/ppermute | solution.py:211
  18.0 2.0 %collective-permute-start.7 = (bf16[8,2,8192]{2,1,0:T(2,128)(2,1)S(1)}, bf16[8,2,8192]{2,1,0:T(2,128)(2,1)S(1)}, u32[]{:S(2)}, u32[]{:S(2)}) collective-permute-start(bf16[8,2,8192]{2,1,0:T(2,128)(2,1)S(1)} %constant_dynamic-update-slice_fusion), channel_id=1, source_target_pairs={{0,1},{1,0},{2,3},{3,2},{4,5},{5,4},{6,7},{7,6},{8,9},{9,8},{10,11... | collective-permute-start | bytes 786440 | tf_op jit(solution)/shard_map/ppermute | solution.py:211
  19.5 1.6 %collective-permute-start.3 = (bf16[8,2,8192]{2,1,0:T(2,128)(2,1)S(1)}, bf16[8,2,8192]{2,1,0:T(2,128)(2,1)S(1)}, u32[]{:S(2)}, u32[]{:S(2)}) collective-permute-start(bf16[8,2,8192]{2,1,0:T(2,128)(2,1)S(1)} %constant_dynamic-update-slice_fusion.3), channel_id=1, source_target_pairs={{0,1},{1,0},{2,3},{3,2},{4,5},{5,4},{6,7},{7,6},{8,9},{9,8},{10,11... | collective-permute-start | bytes 786440 | tf_op jit(solution)/shard_map/ppermute | solution.py:211
  33.2 2.3 %collective-permute-start.8 = (bf16[2,16,8192]{2,1,0:T(8,128)(2,1)S(1)}, bf16[2,16,8192]{2,1,0:T(8,128)(2,1)S(1)}, u32[]{:S(2)}, u32[]{:S(2)}) collective-permute-start(bf16[2,16,8192]{2,1,0:T(8,128)(2,1)S(1)} %get-tuple-element.38), channel_id=1, source_target_pairs={{0,1},{1,0},{2,3},{3,2},{4,5},{5,4},{6,7},{7,6},{8,9},{9,8},{10,11... | collective-permute-start | bytes 1572872 | tf_op jit(solution)/shard_map/ppermute | solution.py:211
  35.7 6.4 %collective-permute-start.9 = (bf16[2,8,8192]{2,1,0:T(8,128)(2,1)S(1)}, bf16[2,8,8192]{2,1,0:T(8,128)(2,1)S(1)}, u32[]{:S(2)}, u32[]{:S(2)}) collective-permute-start(bf16[2,8,8192]{2,1,0:T(8,128)(2,1)S(1)} %slice.73.refs_3_), channel_id=1, source_target_pairs={{0,2},{1,5},{2,0},{3,7},{4,6},{5,1},{6,4},{7,3},{8,10},{9,13},{10,... | collective-permute-start | bytes 786440 | tf_op jit(solution)/shard_map/ppermute | solution.py:211
  42.2 5.3 %collective-permute-start.10 = (bf16[2,4,8192]{2,1,0:T(4,128)(2,1)S(1)}, bf16[2,4,8192]{2,1,0:T(4,128)(2,1)S(1)}, u32[]{:S(2)}, u32[]{:S(2)}) collective-permute-start(bf16[2,4,8192]{2,1,0:T(4,128)(2,1)S(1)} %slice.74.refs_5_), channel_id=1, source_target_pairs={{0,4},{1,3},{2,6},{3,1},{4,0},{5,7},{6,2},{7,5},{8,12},{9,11},{10,... | collective-permute-start | bytes 393224 | tf_op jit(solution)/shard_map/ppermute | solution.py:211
  47.7 5.2 %collective-permute-start.11 = (bf16[2,2,8192]{2,1,0:T(2,128)(2,1)S(1)}, bf16[2,2,8192]{2,1,0:T(2,128)(2,1)S(1)}, u32[]{:S(2)}, u32[]{:S(2)}) collective-permute-start(bf16[2,2,8192]{2,1,0:T(2,128)(2,1)S(1)} %slice.75.refs_5_), channel_id=1, source_target_pairs={{0,8},{1,9},{2,10},{3,11},{4,12},{5,13},{6,14},{7,15},{8,0},{9,1},... | collective-permute-start | bytes 196616 | tf_op jit(solution)/shard_map/ppermute | solution.py:211

commit v3 on v2

--- a/solution.py
+++ b/solution.py
@@ -183,7 +183,7 @@
             for k, (stage, grad) in enumerate(zip(stages, grad_refs))
         ]
 
-    group = max(k for k in range(1, 6) if count % k == 0)
+    group = max(k for k in range(1, 5) if count % k == 0)
 
     def step(g, carry):
         some = [g * group + k for k in range(group)]
@@ -310,7 +310,7 @@
         )(live, pad, factor, *earlier, *after)
 
     near = max(1, blocks // 6)
-    middle = near + (blocks - near + 1) // 2
+    middle = min(blocks - 1, near + (3 * (blocks - near) + 4) // 5)
     cuts = {0: (0, near), 2: (near, middle), 3: (middle, blocks)}
     gate_up, down_grad, after = [], None, []
     for i, bits in enumerate([cores] + x_hops[::-1]):

time: 54.1 us -> 54.5 us (level); the launches traced: 53.6 us -> 54.7 us
  waiting for transfers between devices: 7.34 us -> 10 us
  starting transfers between devices: 17.4 us -> 15.2 us
  Pallas kernels: 25.5 us -> 26.1 us
    ppermute x12, waiting for transfers between devices: 7.34 us -> 10 us  [swap(): return lax.ppermute(value, 'col', [(j, j ^ bits[j % 2]) for j in range(n)])]
    ppermute x12, starting transfers between devices: 17.4 us -> 15.2 us  [swap(): return lax.ppermute(value, 'col', [(j, j ^ bits[j % 2]) for j in range(n)])]
    pallas_call x1, Pallas kernels: 12.1 us -> 12.6 us  [local(): pl.pallas_call(layer_kernel, in_specs=[smem] * 4 + [vmem] * 4 + [hbm] * 3...]
  transfers between devices with their start and end apart: 12 -> 12, of which waited for: 9 -> 10; matrix products, arithmetic and copies ran while one was open for 3% -> 2% of each run, Pallas kernels for 25% -> 25%
where the time goes in v3:
time: 54.5 us; the launch traced here: 54.7 us
  Pallas kernels  26.1 us (48%)
  starting transfers between devices  15.2 us (28%)
  waiting for transfers between devices  10 us (18%)
  local copies, waits for them, and re-layouts  2.28 us (4%)
  between operations  0.84 us (2%)
    ppermute x12, starting transfers between devices, swap(): return lax.ppermute(value, 'col', [(j, j ^ bits[j % 2]) for j in range(n)])  15.2 us
    pallas_call x1, Pallas kernels, local(): pl.pallas_call(layer_kernel, in_specs=[smem] * 4 + [vmem] * 4 + [hbm] * 3...  12.6 us
    pallas_call x4, Pallas kernels, grads(): pl.pallas_call(functools.partial(grad_kernel, products, first, count, out...  12.1 us
    ppermute x12, waiting for transfers between devices, swap(): return lax.ppermute(value, 'col', [(j, j ^ bits[j % 2]) for j in range(n)])  10 us
    pallas_call x1, Pallas kernels, local(): pl.pallas_call(functools.partial(seed_kernel, width // blk), in_specs=[sm...  1.41 us
  transfers between devices with their start and end apart: 12, of which 10 were waited for; matrix products, arithmetic and copies ran while one was open for 2% of the time, Pallas kernels for 25%

profile of v3, /device:TPU:0, one launch (start us, length us, event | category | flops | bytes accessed | tf_op | source)
XLA Modules:
  0.0 54.7 jit_solution(15326722438142934450)
XLA Ops:
  0.6 4.1 %collective-permute-start.4 = (bf16[1,2,8192]{2,1,0:T(2,128)(2,1)}, bf16[1,2,8192]{2,1,0:T(2,128)(2,1)S(1)}, u32[]{:S(2)}, u32[]{:S(2)}) collective-permute-start(bf16[1,2,8192]{2,1,0:T(2,128)(2,1)} %bitcast.18), channel_id=1, source_target_pairs={{0,8},{1,9},{2,10},{3,11},{4,12},{5,13},{6,14},{7,15},{8,0},{9,1},... | collective-permute-start | bytes 98312 | tf_op jit(solution)/shard_map/ppermute | solution.py:211
  4.8 1.4 %seed.1 = (s32[13,20]{1,0:T(8,128)S(4)}, s32[69]{0:T(128)S(4)}, s32[69]{0:T(128)S(4)}, s32[1]{0:T(128)S(4)}, bf16[8,2,8192]{2,1,0:T(2,128)(2,1)S(1)}, /*index=5*/bf16[8,2,8192]{2,1,0:T(2,128)(2,1)S(1)}) custom-call(s32[12,20]{1,0:T(8,128)} %rows_ref.1, s32[12]{0:T(128)} %count_ref.1, bf16[2,8192]{1,0:T(2,128)(2,1)} %x_ref.1, bf16[2,8192]{1,0:T(2,128)(2,1)} %dy_ref.1), custom_call_target="tpu_custom_call" | custom-call | tf_op jit(solution)/shard_map/seed/pallas_call | solution.py:250
  6.2 1.0 %collective-permute-done.4 = bf16[1,2,8192]{2,1,0:T(2,128)(2,1)S(1)} collective-permute-done((bf16[1,2,8192]{2,1,0:T(2,128)(2,1)}, bf16[1,2,8192]{2,1,0:T(2,128)(2,1)S(1)}, u32[]{:S(2)}, u32[]{:S(2)}) %collective-permute-start.4) | collective-permute-done | bytes 32800 | tf_op jit(solution)/shard_map/ppermute | solution.py:211
  7.3 1.8 %collective-permute-start.5 = (bf16[2,2,8192]{2,1,0:T(2,128)(2,1)S(1)}, bf16[2,2,8192]{2,1,0:T(2,128)(2,1)S(1)}, u32[]{:S(2)}, u32[]{:S(2)}) collective-permute-start(bf16[2,2,8192]{2,1,0:T(2,128)(2,1)S(1)} %slice.53), channel_id=1, source_target_pairs={{0,2},{1,5},{2,0},{3,7},{4,6},{5,1},{6,4},{7,3},{8,10},{9,13},{10,... | collective-permute-start | bytes 196616 | tf_op jit(solution)/shard_map/ppermute | solution.py:211
  9.1 0.7 %collective-permute-done = bf16[1,2,8192]{2,1,0:T(2,128)(2,1)S(1)} collective-permute-done((bf16[1,2,8192]{2,1,0:T(2,128)(2,1)}, bf16[1,2,8192]{2,1,0:T(2,128)(2,1)S(1)}, u32[]{:S(2)}, u32[]{:S(2)}) %collective-permute-start) | collective-permute-done | bytes 32800 | tf_op jit(solution)/shard_map/ppermute | solution.py:211
  9.8 1.6 %collective-permute-start.1 = (bf16[2,2,8192]{2,1,0:T(2,128)(2,1)S(1)}, bf16[2,2,8192]{2,1,0:T(2,128)(2,1)S(1)}, u32[]{:S(2)}, u32[]{:S(2)}) collective-permute-start(bf16[2,2,8192]{2,1,0:T(2,128)(2,1)S(1)} %slice.51), channel_id=1, source_target_pairs={{0,4},{1,3},{2,6},{3,1},{4,0},{5,7},{6,2},{7,5},{8,12},{9,11},{10,... | collective-permute-start | bytes 196616 | tf_op jit(solution)/shard_map/ppermute | solution.py:211
  11.5 0.6 %collective-permute-done.5 = bf16[2,2,8192]{2,1,0:T(2,128)(2,1)S(1)} collective-permute-done((bf16[2,2,8192]{2,1,0:T(2,128)(2,1)S(1)}, bf16[2,2,8192]{2,1,0:T(2,128)(2,1)S(1)}, u32[]{:S(2)}, u32[]{:S(2)}) %collective-permute-start.5) | collective-permute-done | bytes 65568 | tf_op jit(solution)/shard_map/ppermute | solution.py:211
  12.3 1.8 %collective-permute-start.6 = (bf16[4,2,8192]{2,1,0:T(2,128)(2,1)S(1)}, bf16[4,2,8192]{2,1,0:T(2,128)(2,1)S(1)}, u32[]{:S(2)}, u32[]{:S(2)}) collective-permute-start(bf16[4,2,8192]{2,1,0:T(2,128)(2,1)S(1)} %slice.54), channel_id=1, source_target_pairs={{0,4},{1,3},{2,6},{3,1},{4,0},{5,7},{6,2},{7,5},{8,12},{9,11},{10,... | collective-permute-start | bytes 393224 | tf_op jit(solution)/shard_map/ppermute | solution.py:211
  14.3 1.6 %collective-permute-start.2 = (bf16[4,2,8192]{2,1,0:T(2,128)(2,1)S(1)}, bf16[4,2,8192]{2,1,0:T(2,128)(2,1)S(1)}, u32[]{:S(2)}, u32[]{:S(2)}) collective-permute-start(bf16[4,2,8192]{2,1,0:T(2,128)(2,1)S(1)} %slice.52), channel_id=1, source_target_pairs={{0,2},{1,5},{2,0},{3,7},{4,6},{5,1},{6,4},{7,3},{8,10},{9,13},{10,... | collective-permute-start | bytes 393224 | tf_op jit(solution)/shard_map/ppermute | solution.py:211
  15.9 1.9 %collective-permute-done.6 = bf16[4,2,8192]{2,1,0:T(2,128)(2,1)S(1)} collective-permute-done((bf16[4,2,8192]{2,1,0:T(2,128)(2,1)S(1)}, bf16[4,2,8192]{2,1,0:T(2,128)(2,1)S(1)}, u32[]{:S(2)}, u32[]{:S(2)}) %collective-permute-start.6) | collective-permute-done | bytes 131104 | tf_op jit(solution)/shard_map/ppermute | solution.py:211
  17.9 0.1 constant_dynamic-update-slice_fusion
  18.0 1.3 %collective-permute-done.2 = bf16[4,2,8192]{2,1,0:T(2,128)(2,1)S(1)} collective-permute-done((bf16[4,2,8192]{2,1,0:T(2,128)(2,1)S(1)}, bf16[4,2,8192]{2,1,0:T(2,128)(2,1)S(1)}, u32[]{:S(2)}, u32[]{:S(2)}) %collective-permute-start.2) | collective-permute-done | bytes 131104 | tf_op jit(solution)/shard_map/ppermute | solution.py:211
  19.4 0.1 constant_dynamic-update-slice_fusion.3
  19.6 0.1 reshape.28.x_near
  19.7 0.2 copy.21
  19.9 0.1 reshape.31.dy_near
  20.0 0.2 copy.20
  20.2 0.1 reshape.33.dy_far
  20.3 0.8 %collective-permute-done.3 = bf16[8,2,8192]{2,1,0:T(2,128)(2,1)S(1)} collective-permute-done((bf16[8,2,8192]{2,1,0:T(2,128)(2,1)S(1)}, bf16[8,2,8192]{2,1,0:T(2,128)(2,1)S(1)}, u32[]{:S(2)}, u32[]{:S(2)}) %collective-permute-start.3) | collective-permute-done | bytes 262176 | tf_op jit(solution)/shard_map/ppermute | solution.py:211
  21.1 0.1 reshape.29.x_far
  21.2 12.6 %layer.1 = (bf16[13,32,128]{2,1,0:T(8,128)(2,1)S(1)}, bf16[13,32,256]{2,1,0:T(8,128)(2,1)S(1)}, bf16[65,32,128]{2,1,0:T(8,128)(2,1)S(1)}, bf16[65,32,128]{2,1,0:...) custom-call(s32[13,20]{1,0:T(8,128)S(4)} %get-tuple-element.31.live_ref.refs_0_, ...), custom_call_target="tpu_custom_call" | custom-call | flops 1509949440 | bytes 23592960 | tf_op jit(solution)/shard_map/layer/pallas_call | solution.py:273
  33.8 0.4 collective-permute-start.8
  34.2 1.9 %gate_up_grad.3 = (bf16[12,20,128,128]{3,2,1,0:T(8,128)(2,1)}, bf16[12,20,128,128]{3,2,1,0:T(8,128)(2,1)}) custom-call(s32[13,20]{1,0:T(8,128)S(4)} %get-tuple-element.31.live_ref.refs_0_, bf16[65,32,128]{2,1,0:T(8,128)(2,1)S(1)} %get-tuple-element.39.refs_1_, bf16[13,32,256]{2,1,0:T(8,128)(2,1)S(1)} %get-tuple-element.40.refs_2_), custom_call_target="tpu_custom_call" | custom-call | flops 83886080 | bytes 2621440 | tf_op jit(solution)/shard_map/gate_up_grad/pallas_call | solution.py:297
  36.3 1.7 %collective-permute-start.9 = (bf16[2,8,8192]{2,1,0:T(8,128)(2,1)S(1)}, bf16[2,8,8192]{2,1,0:T(8,128)(2,1)S(1)}, u32[]{:S(2)}, u32[]{:S(2)}) collective-permute-start(bf16[2,8,8192]{2,1,0:T(8,128)(2,1)S(1)} %slice.73.refs_3_), channel_id=1, source_target_pairs={{0,2},{1,5},{2,0},{3,7},{4,6},{5,1},{6,4},{7,3},{8,10},{9,13},{10,... | collective-permute-start | bytes 786440 | tf_op jit(solution)/shard_map/ppermute | solution.py:211
  38.0 3.6 %down_grad.1 = bf16[12,20,128,128]{3,2,1,0:T(8,128)(2,1)} custom-call(s32[13,20]{1,0:T(8,128)S(4)} %get-tuple-element.31.live_ref.refs_0_, bf16[65,32,128]{2,1,0:T(8,128)(2,1)S(1)} %get-tuple-element.44.refs_1_, bf16[13,32,128]{2,1,0:T(8,128)(2,1)S(1)} %get-tuple-element.45.refs_2_, bf16[2,8,8192]{2,1,0:T(8,128)(2,1)S(1)} %slice.73.refs_3_), custom_call_target="tpu_custom_call" | custom-call | flops 251658240 | bytes 7864320 | tf_op jit(solution)/shard_map/down_grad/pallas_call | solution.py:297
  41.7 1.0 %collective-permute-done.9 = bf16[2,8,8192]{2,1,0:T(8,128)(2,1)S(1)} collective-permute-done((bf16[2,8,8192]{2,1,0:T(8,128)(2,1)S(1)}, bf16[2,8,8192]{2,1,0:T(8,128)(2,1)S(1)}, u32[]{:S(2)}, u32[]{:S(2)}) %collective-permute-start.9) | collective-permute-done | bytes 262176 | tf_op jit(solution)/shard_map/ppermute | solution.py:211
  42.9 3.7 %gate_up_grad.4 = (bf16[12,20,128,128]{3,2,1,0:T(8,128)(2,1)}, bf16[12,20,128,128]{3,2,1,0:T(8,128)(2,1)}) custom-call(s32[13,20]{1,0:T(8,128)S(4)} %get-tuple-element.31.live_ref.refs_0_, bf16[65,32,128]{2,1,0:T(8,128)(2,1)S(1)} %get-tuple-element.39.refs_1_, ...), custom_call_target="tpu_custom_call", output_to_operand_aliasing={{0}: (3, {}), {1}: (4, {})} | custom-call | flops 251658240 | bytes 7864320 | tf_op jit(solution)/shard_map/gate_up_grad/pallas_call | solution.py:297
  46.6 1.3 %collective-permute-done.10 = bf16[2,4,8192]{2,1,0:T(4,128)(2,1)S(1)} collective-permute-done((bf16[2,4,8192]{2,1,0:T(4,128)(2,1)S(1)}, bf16[2,4,8192]{2,1,0:T(4,128)(2,1)S(1)}, u32[]{:S(2)}, u32[]{:S(2)}) %collective-permute-start.10) | collective-permute-done | bytes 131104 | tf_op jit(solution)/shard_map/ppermute | solution.py:211
  48.0 1.8 %collective-permute-start.11 = (bf16[2,2,8192]{2,1,0:T(2,128)(2,1)S(1)}, bf16[2,2,8192]{2,1,0:T(2,128)(2,1)S(1)}, u32[]{:S(2)}, u32[]{:S(2)}) collective-permute-start(bf16[2,2,8192]{2,1,0:T(2,128)(2,1)S(1)} %slice.75.refs_5_), channel_id=1, source_target_pairs={{0,8},{1,9},{2,10},{3,11},{4,12},{5,13},{6,14},{7,15},{8,0},{9,1},... | collective-permute-start | bytes 196616 | tf_op jit(solution)/shard_map/ppermute | solution.py:211
  49.8 2.8 %gate_up_grad.5 = (bf16[12,20,128,128]{3,2,1,0:T(8,128)(2,1)}, bf16[12,20,128,128]{3,2,1,0:T(8,128)(2,1)}) custom-call(s32[13,20]{1,0:T(8,128)S(4)} %get-tuple-element.31.live_ref.refs_0_, bf16[65,32,128]{2,1,0:T(8,128)(2,1)S(1)} %get-tuple-element.39.refs_1_, ...), custom_call_target="tpu_custom_call", output_to_operand_aliasing={{0}: (3, {}), {1}: (4, {})} | custom-call | flops 167772160 | bytes 5242880 | tf_op jit(solution)/shard_map/gate_up_grad/pallas_call | solution.py:297
  52.6 1.3 %collective-permute-done.11 = bf16[2,2,8192]{2,1,0:T(2,128)(2,1)S(1)} collective-permute-done((bf16[2,2,8192]{2,1,0:T(2,128)(2,1)S(1)}, bf16[2,2,8192]{2,1,0:T(2,128)(2,1)S(1)}, u32[]{:S(2)}, u32[]{:S(2)}) %collective-permute-start.11) | collective-permute-done | bytes 65568 | tf_op jit(solution)/shard_map/ppermute | solution.py:211
  54.0 0.7 %slice_bitcast_fusion = (bf16[2,8192]{1,0:T(2,128)(2,1)}, bf16[2,8192]{1,0:T(2,128)(2,1)}) fusion(bf16[2,2,8192]{2,1,0:T(2,128)(2,1)S(1)} %fusion), kind=kLoop, calls=%fused_computation.10 | loop fusion | bytes 131072 | tf_op jit(solution)/shard_map/squeeze | solution.py:341
  (22 shorter events, 1.2 us)
Async XLA Ops:
  0.6 6.6 %collective-permute-start.4 = (bf16[1,2,8192]{2,1,0:T(2,128)(2,1)}, bf16[1,2,8192]{2,1,0:T(2,128)(2,1)S(1)}, u32[]{:S(2)}, u32[]{:S(2)}) collective-permute-start(bf16[1,2,8192]{2,1,0:T(2,128)(2,1)} %bitcast.18), channel_id=1, source_target_pairs={{0,8},{1,9},{2,10},{3,11},{4,12},{5,13},{6,14},{7,15},{8,0},{9,1},... | collective-permute-start | bytes 98312 | tf_op jit(solution)/shard_map/ppermute | solution.py:211
  4.7 5.0 %collective-permute-start = (bf16[1,2,8192]{2,1,0:T(2,128)(2,1)}, bf16[1,2,8192]{2,1,0:T(2,128)(2,1)S(1)}, u32[]{:S(2)}, u32[]{:S(2)}) collective-permute-start(bf16[1,2,8192]{2,1,0:T(2,128)(2,1)} %bitcast.19), channel_id=1, source_target_pairs={{0,8},{1,9},{2,10},{3,11},{4,12},{5,13},{6,14},{7,15},{8,0},{9,1},... | collective-permute-start | bytes 98312 | tf_op jit(solution)/shard_map/ppermute | solution.py:211
  7.3 4.8 %collective-permute-start.5 = (bf16[2,2,8192]{2,1,0:T(2,128)(2,1)S(1)}, bf16[2,2,8192]{2,1,0:T(2,128)(2,1)S(1)}, u32[]{:S(2)}, u32[]{:S(2)}) collective-permute-start(bf16[2,2,8192]{2,1,0:T(2,128)(2,1)S(1)} %slice.53), channel_id=1, source_target_pairs={{0,2},{1,5},{2,0},{3,7},{4,6},{5,1},{6,4},{7,3},{8,10},{9,13},{10,... | collective-permute-start | bytes 196616 | tf_op jit(solution)/shard_map/ppermute | solution.py:211
  9.8 4.3 %collective-permute-start.1 = (bf16[2,2,8192]{2,1,0:T(2,128)(2,1)S(1)}, bf16[2,2,8192]{2,1,0:T(2,128)(2,1)S(1)}, u32[]{:S(2)}, u32[]{:S(2)}) collective-permute-start(bf16[2,2,8192]{2,1,0:T(2,128)(2,1)S(1)} %slice.51), channel_id=1, source_target_pairs={{0,4},{1,3},{2,6},{3,1},{4,0},{5,7},{6,2},{7,5},{8,12},{9,11},{10,... | collective-permute-start | bytes 196616 | tf_op jit(solution)/shard_map/ppermute | solution.py:211
  12.3 5.6 %collective-permute-start.6 = (bf16[4,2,8192]{2,1,0:T(2,128)(2,1)S(1)}, bf16[4,2,8192]{2,1,0:T(2,128)(2,1)S(1)}, u32[]{:S(2)}, u32[]{:S(2)}) collective-permute-start(bf16[4,2,8192]{2,1,0:T(2,128)(2,1)S(1)} %slice.54), channel_id=1, source_target_pairs={{0,4},{1,3},{2,6},{3,1},{4,0},{5,7},{6,2},{7,5},{8,12},{9,11},{10,... | collective-permute-start | bytes 393224 | tf_op jit(solution)/shard_map/ppermute | solution.py:211
  14.3 5.0 %collective-permute-start.2 = (bf16[4,2,8192]{2,1,0:T(2,128)(2,1)S(1)}, bf16[4,2,8192]{2,1,0:T(2,128)(2,1)S(1)}, u32[]{:S(2)}, u32[]{:S(2)}) collective-permute-start(bf16[4,2,8192]{2,1,0:T(2,128)(2,1)S(1)} %slice.52), channel_id=1, source_target_pairs={{0,2},{1,5},{2,0},{3,7},{4,6},{5,1},{6,4},{7,3},{8,10},{9,13},{10,... | collective-permute-start | bytes 393224 | tf_op jit(solution)/shard_map/ppermute | solution.py:211
  18.0 2.0 %collective-permute-start.7 = (bf16[8,2,8192]{2,1,0:T(2,128)(2,1)S(1)}, bf16[8,2,8192]{2,1,0:T(2,128)(2,1)S(1)}, u32[]{:S(2)}, u32[]{:S(2)}) collective-permute-start(bf16[8,2,8192]{2,1,0:T(2,128)(2,1)S(1)} %constant_dynamic-update-slice_fusion), channel_id=1, source_target_pairs={{0,1},{1,0},{2,3},{3,2},{4,5},{5,4},{6,7},{7,6},{8,9},{9,8},{10,11... | collective-permute-start | bytes 786440 | tf_op jit(solution)/shard_map/ppermute | solution.py:211
  19.5 1.6 %collective-permute-start.3 = (bf16[8,2,8192]{2,1,0:T(2,128)(2,1)S(1)}, bf16[8,2,8192]{2,1,0:T(2,128)(2,1)S(1)}, u32[]{:S(2)}, u32[]{:S(2)}) collective-permute-start(bf16[8,2,8192]{2,1,0:T(2,128)(2,1)S(1)} %constant_dynamic-update-slice_fusion.3), channel_id=1, source_target_pairs={{0,1},{1,0},{2,3},{3,2},{4,5},{5,4},{6,7},{7,6},{8,9},{9,8},{10,11... | collective-permute-start | bytes 786440 | tf_op jit(solution)/shard_map/ppermute | solution.py:211
  33.8 2.3 %collective-permute-start.8 = (bf16[2,16,8192]{2,1,0:T(8,128)(2,1)S(1)}, bf16[2,16,8192]{2,1,0:T(8,128)(2,1)S(1)}, u32[]{:S(2)}, u32[]{:S(2)}) collective-permute-start(bf16[2,16,8192]{2,1,0:T(8,128)(2,1)S(1)} %get-tuple-element.38), channel_id=1, source_target_pairs={{0,1},{1,0},{2,3},{3,2},{4,5},{5,4},{6,7},{7,6},{8,9},{9,8},{10,11... | collective-permute-start | bytes 1572872 | tf_op jit(solution)/shard_map/ppermute | solution.py:211
  36.3 6.4 %collective-permute-start.9 = (bf16[2,8,8192]{2,1,0:T(8,128)(2,1)S(1)}, bf16[2,8,8192]{2,1,0:T(8,128)(2,1)S(1)}, u32[]{:S(2)}, u32[]{:S(2)}) collective-permute-start(bf16[2,8,8192]{2,1,0:T(8,128)(2,1)S(1)} %slice.73.refs_3_), channel_id=1, source_target_pairs={{0,2},{1,5},{2,0},{3,7},{4,6},{5,1},{6,4},{7,3},{8,10},{9,13},{10,... | collective-permute-start | bytes 786440 | tf_op jit(solution)/shard_map/ppermute | solution.py:211
  42.8 5.0 %collective-permute-start.10 = (bf16[2,4,8192]{2,1,0:T(4,128)(2,1)S(1)}, bf16[2,4,8192]{2,1,0:T(4,128)(2,1)S(1)}, u32[]{:S(2)}, u32[]{:S(2)}) collective-permute-start(bf16[2,4,8192]{2,1,0:T(4,128)(2,1)S(1)} %slice.74.refs_5_), channel_id=1, source_target_pairs={{0,4},{1,3},{2,6},{3,1},{4,0},{5,7},{6,2},{7,5},{8,12},{9,11},{10,... | collective-permute-start | bytes 393224 | tf_op jit(solution)/shard_map/ppermute | solution.py:211
  48.0 5.9 %collective-permute-start.11 = (bf16[2,2,8192]{2,1,0:T(2,128)(2,1)S(1)}, bf16[2,2,8192]{2,1,0:T(2,128)(2,1)S(1)}, u32[]{:S(2)}, u32[]{:S(2)}) collective-permute-start(bf16[2,2,8192]{2,1,0:T(2,128)(2,1)S(1)} %slice.75.refs_5_), channel_id=1, source_target_pairs={{0,8},{1,9},{2,10},{3,11},{4,12},{5,13},{6,14},{7,15},{8,0},{9,1},... | collective-permute-start | bytes 196616 | tf_op jit(solution)/shard_map/ppermute | solution.py:211

commit v4 on v3

--- a/solution.py
+++ b/solution.py
@@ -309,36 +309,31 @@
             name=name,
         )(live, pad, factor, *earlier, *after)
 
-    near = max(1, blocks // 6)
-    middle = min(blocks - 1, near + (3 * (blocks - near) + 4) // 5)
-    cuts = {0: (0, near), 2: (near, middle), 3: (middle, blocks)}
-    gate_up, down_grad, after = [], None, []
+    near = max(1, blocks // 12)
+    beside = near + blocks // 12
+    middle = min(blocks - 1, beside + (3 * (blocks - beside) + 4) // 5)
+    cuts = {0: (0, near), 1: (near, beside), 2: (beside, middle), 3: (middle, blocks)}
+    gate_up, down_grad, after = [], [], []
     for i, bits in enumerate([cores] + x_hops[::-1]):
         got = swap(send, bits, n)
-        done = []
         if i == 1:
-            (down_grad,) = grads(
+            down_grad = grads(
                 down_products, dypad, hidden, 0, blocks, 1, [], after, "down_grad"
             )
-            done = [down_grad]
-        elif i in cuts:
-            first, last = cuts[i]
+        first, last = cuts.get(i, (0, 0))
+        if first < last:
             gate_up = grads(
                 gate_up_products, xpad, d, first, last - first, 2, gate_up, after, "gate_up_grad"
             )
-            done = gate_up
         total = keep + got.astype(jnp.float32)
         if i < len(x_hops):
             half = total.shape[1] // 2
             keep, send = total[:, :half], total[:, half:].astype(jnp.bfloat16)
-            send, done = lax.optimization_barrier((send, done))
+            send, done = lax.optimization_barrier((send, (gate_up, down_grad)))
             after = [send]
-            if i == 1:
-                (down_grad,) = done
-            elif i in cuts:
-                gate_up = done
+            gate_up, down_grad = done
     total = total.astype(jnp.bfloat16)
-    return total[0], total[1], gate_up[0], gate_up[1], down_grad
+    return total[0], total[1], gate_up[0], gate_up[1], down_grad[0]
 
 
 def solution(mesh):

time: 54.5 us -> 54.8 us (level)
  starting transfers between devices: 15.2 us -> 18.5 us
  waiting for transfers between devices: 10 us -> 7.53 us
  Pallas kernels: 26.1 us -> 25.2 us
    ppermute x12, starting transfers between devices: 15.2 us -> 18.5 us  [swap(): return lax.ppermute(value, 'col', [(j, j ^ bits[j % 2]) for j in range(n)])]
    ppermute x12, waiting for transfers between devices: 10 us -> 7.53 us  [swap(): return lax.ppermute(value, 'col', [(j, j ^ bits[j % 2]) for j in range(n)])]
    pallas_call x1, Pallas kernels: 12.6 us -> 10.7 us  [local(): pl.pallas_call(layer_kernel, in_specs=[smem] * 4 + [vmem] * 4 + [hbm] * 3...]
    pallas_call x4 -> x5, Pallas kernels: 12.1 us -> 13.1 us  [grads(): pl.pallas_call(functools.partial(grad_kernel, products, first, count, out...]
  transfers between devices with their start and end apart: 12 -> 12, of which waited for: 10 -> 10; matrix products, arithmetic and copies ran while one was open for 2% -> 2% of each run, Pallas kernels for 25% -> 27%
where the time goes in v4:
time: 54.8 us; the launch traced here: 54.5 us
  Pallas kernels  25.2 us (46%)
  starting transfers between devices  18.5 us (34%)
  waiting for transfers between devices  7.53 us (14%)
  local copies, waits for them, and re-layouts  2.28 us (4%)
  between operations  0.84 us (2%)
    ppermute x12, starting transfers between devices, swap(): return lax.ppermute(value, 'col', [(j, j ^ bits[j % 2]) for j in range(n)])  18.5 us
    pallas_call x5, Pallas kernels, grads(): pl.pallas_call(functools.partial(grad_kernel, products, first, count, out...  13.1 us
    pallas_call x1, Pallas kernels, local(): pl.pallas_call(layer_kernel, in_specs=[smem] * 4 + [vmem] * 4 + [hbm] * 3...  10.7 us
    ppermute x12, waiting for transfers between devices, swap(): return lax.ppermute(value, 'col', [(j, j ^ bits[j % 2]) for j in range(n)])  7.53 us
    pallas_call x1, Pallas kernels, local(): pl.pallas_call(functools.partial(seed_kernel, width // blk), in_specs=[sm...  1.41 us
  transfers between devices with their start and end apart: 12, of which 10 were waited for; matrix products, arithmetic and copies ran while one was open for 2% of the time, Pallas kernels for 27%

profile of v4, /device:TPU:0, one launch (start us, length us, event | category | flops | bytes accessed | tf_op | source)
XLA Modules:
  0.0 54.5 jit_solution(2893566745701995052)
XLA Ops:
  0.6 4.1 %collective-permute-start.4 = (bf16[1,2,8192]{2,1,0:T(2,128)(2,1)}, bf16[1,2,8192]{2,1,0:T(2,128)(2,1)S(1)}, u32[]{:S(2)}, u32[]{:S(2)}) collective-permute-start(bf16[1,2,8192]{2,1,0:T(2,128)(2,1)} %bitcast.18), channel_id=1, source_target_pairs={{0,8},{1,9},{2,10},{3,11},{4,12},{5,13},{6,14},{7,15},{8,0},{9,1},... | collective-permute-start | bytes 98312 | tf_op jit(solution)/shard_map/ppermute | solution.py:211
  4.8 1.4 %seed.1 = (s32[13,20]{1,0:T(8,128)S(4)}, s32[69]{0:T(128)S(4)}, s32[69]{0:T(128)S(4)}, s32[1]{0:T(128)S(4)}, bf16[8,2,8192]{2,1,0:T(2,128)(2,1)S(1)}, /*index=5*/bf16[8,2,8192]{2,1,0:T(2,128)(2,1)S(1)}) custom-call(s32[12,20]{1,0:T(8,128)} %rows_ref.1, s32[12]{0:T(128)} %count_ref.1, bf16[2,8192]{1,0:T(2,128)(2,1)} %x_ref.1, bf16[2,8192]{1,0:T(2,128)(2,1)} %dy_ref.1), custom_call_target="tpu_custom_call" | custom-call | tf_op jit(solution)/shard_map/seed/pallas_call | solution.py:250
  6.2 1.0 %collective-permute-done.4 = bf16[1,2,8192]{2,1,0:T(2,128)(2,1)S(1)} collective-permute-done((bf16[1,2,8192]{2,1,0:T(2,128)(2,1)}, bf16[1,2,8192]{2,1,0:T(2,128)(2,1)S(1)}, u32[]{:S(2)}, u32[]{:S(2)}) %collective-permute-start.4) | collective-permute-done | bytes 32800 | tf_op jit(solution)/shard_map/ppermute | solution.py:211
  7.3 1.8 %collective-permute-start.5 = (bf16[2,2,8192]{2,1,0:T(2,128)(2,1)S(1)}, bf16[2,2,8192]{2,1,0:T(2,128)(2,1)S(1)}, u32[]{:S(2)}, u32[]{:S(2)}) collective-permute-start(bf16[2,2,8192]{2,1,0:T(2,128)(2,1)S(1)} %slice.53), channel_id=1, source_target_pairs={{0,2},{1,5},{2,0},{3,7},{4,6},{5,1},{6,4},{7,3},{8,10},{9,13},{10,... | collective-permute-start | bytes 196616 | tf_op jit(solution)/shard_map/ppermute | solution.py:211
  9.1 0.7 %collective-permute-done = bf16[1,2,8192]{2,1,0:T(2,128)(2,1)S(1)} collective-permute-done((bf16[1,2,8192]{2,1,0:T(2,128)(2,1)}, bf16[1,2,8192]{2,1,0:T(2,128)(2,1)S(1)}, u32[]{:S(2)}, u32[]{:S(2)}) %collective-permute-start) | collective-permute-done | bytes 32800 | tf_op jit(solution)/shard_map/ppermute | solution.py:211
  9.8 1.6 %collective-permute-start.1 = (bf16[2,2,8192]{2,1,0:T(2,128)(2,1)S(1)}, bf16[2,2,8192]{2,1,0:T(2,128)(2,1)S(1)}, u32[]{:S(2)}, u32[]{:S(2)}) collective-permute-start(bf16[2,2,8192]{2,1,0:T(2,128)(2,1)S(1)} %slice.51), channel_id=1, source_target_pairs={{0,4},{1,3},{2,6},{3,1},{4,0},{5,7},{6,2},{7,5},{8,12},{9,11},{10,... | collective-permute-start | bytes 196616 | tf_op jit(solution)/shard_map/ppermute | solution.py:211
  11.5 0.6 %collective-permute-done.5 = bf16[2,2,8192]{2,1,0:T(2,128)(2,1)S(1)} collective-permute-done((bf16[2,2,8192]{2,1,0:T(2,128)(2,1)S(1)}, bf16[2,2,8192]{2,1,0:T(2,128)(2,1)S(1)}, u32[]{:S(2)}, u32[]{:S(2)}) %collective-permute-start.5) | collective-permute-done | bytes 65568 | tf_op jit(solution)/shard_map/ppermute | solution.py:211
  12.3 1.8 %collective-permute-start.6 = (bf16[4,2,8192]{2,1,0:T(2,128)(2,1)S(1)}, bf16[4,2,8192]{2,1,0:T(2,128)(2,1)S(1)}, u32[]{:S(2)}, u32[]{:S(2)}) collective-permute-start(bf16[4,2,8192]{2,1,0:T(2,128)(2,1)S(1)} %slice.54), channel_id=1, source_target_pairs={{0,4},{1,3},{2,6},{3,1},{4,0},{5,7},{6,2},{7,5},{8,12},{9,11},{10,... | collective-permute-start | bytes 393224 | tf_op jit(solution)/shard_map/ppermute | solution.py:211
  14.3 1.6 %collective-permute-start.2 = (bf16[4,2,8192]{2,1,0:T(2,128)(2,1)S(1)}, bf16[4,2,8192]{2,1,0:T(2,128)(2,1)S(1)}, u32[]{:S(2)}, u32[]{:S(2)}) collective-permute-start(bf16[4,2,8192]{2,1,0:T(2,128)(2,1)S(1)} %slice.52), channel_id=1, source_target_pairs={{0,2},{1,5},{2,0},{3,7},{4,6},{5,1},{6,4},{7,3},{8,10},{9,13},{10,... | collective-permute-start | bytes 393224 | tf_op jit(solution)/shard_map/ppermute | solution.py:211
  15.9 1.9 %collective-permute-done.6 = bf16[4,2,8192]{2,1,0:T(2,128)(2,1)S(1)} collective-permute-done((bf16[4,2,8192]{2,1,0:T(2,128)(2,1)S(1)}, bf16[4,2,8192]{2,1,0:T(2,128)(2,1)S(1)}, u32[]{:S(2)}, u32[]{:S(2)}) %collective-permute-start.6) | collective-permute-done | bytes 131104 | tf_op jit(solution)/shard_map/ppermute | solution.py:211
  17.9 0.1 constant_dynamic-update-slice_fusion
  18.0 1.3 %collective-permute-done.2 = bf16[4,2,8192]{2,1,0:T(2,128)(2,1)S(1)} collective-permute-done((bf16[4,2,8192]{2,1,0:T(2,128)(2,1)S(1)}, bf16[4,2,8192]{2,1,0:T(2,128)(2,1)S(1)}, u32[]{:S(2)}, u32[]{:S(2)}) %collective-permute-start.2) | collective-permute-done | bytes 131104 | tf_op jit(solution)/shard_map/ppermute | solution.py:211
  19.4 0.1 constant_dynamic-update-slice_fusion.3
  19.6 0.1 reshape.28.x_near
  19.7 0.2 copy.23
  19.9 0.1 reshape.31.dy_near
  20.0 0.2 copy.22
  20.2 0.1 reshape.33.dy_far
  20.3 0.8 %collective-permute-done.3 = bf16[8,2,8192]{2,1,0:T(2,128)(2,1)S(1)} collective-permute-done((bf16[8,2,8192]{2,1,0:T(2,128)(2,1)S(1)}, bf16[8,2,8192]{2,1,0:T(2,128)(2,1)S(1)}, u32[]{:S(2)}, u32[]{:S(2)}) %collective-permute-start.3) | collective-permute-done | bytes 262176 | tf_op jit(solution)/shard_map/ppermute | solution.py:211
  21.2 10.7 %layer.1 = (bf16[13,32,128]{2,1,0:T(8,128)(2,1)S(1)}, bf16[13,32,256]{2,1,0:T(8,128)(2,1)S(1)}, bf16[65,32,128]{2,1,0:T(8,128)(2,1)S(1)}, bf16[65,32,128]{2,1,0:...) custom-call(s32[13,20]{1,0:T(8,128)S(4)} %get-tuple-element.36.live_ref.refs_0_, ...), custom_call_target="tpu_custom_call" | custom-call | flops 1509949440 | bytes 23592960 | tf_op jit(solution)/shard_map/layer/pallas_call | solution.py:273
  31.9 0.5 collective-permute-start.8
  32.4 1.5 %gate_up_grad.4 = (bf16[12,20,128,128]{3,2,1,0:T(8,128)(2,1)}, bf16[12,20,128,128]{3,2,1,0:T(8,128)(2,1)}) custom-call(s32[13,20]{1,0:T(8,128)S(4)} %get-tuple-element.36.live_ref.refs_0_, bf16[65,32,128]{2,1,0:T(8,128)(2,1)S(1)} %get-tuple-element.44.refs_1_, bf16[13,32,256]{2,1,0:T(8,128)(2,1)S(1)} %get-tuple-element.45.refs_2_), custom_call_target="tpu_custom_call" | custom-call | flops 41943040 | bytes 1310720 | tf_op jit(solution)/shard_map/gate_up_grad/pallas_call | solution.py:297
  34.0 3.2 %collective-permute-start.9 = (bf16[2,8,8192]{2,1,0:T(8,128)(2,1)S(1)}, bf16[2,8,8192]{2,1,0:T(8,128)(2,1)S(1)}, u32[]{:S(2)}, u32[]{:S(2)}) collective-permute-start(bf16[2,8,8192]{2,1,0:T(8,128)(2,1)S(1)} %slice.73.refs_5_.refs_3_), channel_id=1, source_target_pairs={{0,2},{1,5},{2,0},{3,7},{4,6},{5,1},{6,4},{7,3},{8,10},{9,13},{10,... | collective-permute-start | bytes 786440 | tf_op jit(solution)/shard_map/ppermute | solution.py:211
  37.3 1.5 %gate_up_grad.5 = (bf16[12,20,128,128]{3,2,1,0:T(8,128)(2,1)}, bf16[12,20,128,128]{3,2,1,0:T(8,128)(2,1)}) custom-call(s32[13,20]{1,0:T(8,128)S(4)} %get-tuple-element.36.live_ref.refs_0_, bf16[65,32,128]{2,1,0:T(8,128)(2,1)S(1)} %get-tuple-element.44.refs_1_, ...), custom_call_target="tpu_custom_call", output_to_operand_aliasing={{0}: (3, {}), {1}: (4, {})} | custom-call | flops 41943040 | bytes 1310720 | tf_op jit(solution)/shard_map/gate_up_grad/pallas_call | solution.py:297
  38.7 3.6 %down_grad.1 = bf16[12,20,128,128]{3,2,1,0:T(8,128)(2,1)} custom-call(s32[13,20]{1,0:T(8,128)S(4)} %get-tuple-element.36.live_ref.refs_0_, bf16[65,32,128]{2,1,0:T(8,128)(2,1)S(1)} %get-tuple-element.53.refs_1_, bf16[13,32,128]{2,1,0:T(8,128)(2,1)S(1)} %get-tuple-element.54.refs_2_, bf16[2,8,8192]{2,1,0:T(8,128)(2,1)S(1)} %slice.73.refs_5_.refs_3_), custom_call_target="tpu_custom_call" | custom-call | flops 251658240 | bytes 7864320 | tf_op jit(solution)/shard_map/down_grad/pallas_call | solution.py:297
  42.5 1.2 %collective-permute-start.10 = (bf16[2,4,8192]{2,1,0:T(4,128)(2,1)S(1)}, bf16[2,4,8192]{2,1,0:T(4,128)(2,1)S(1)}, u32[]{:S(2)}, u32[]{:S(2)}) collective-permute-start(bf16[2,4,8192]{2,1,0:T(4,128)(2,1)S(1)} %slice.74.refs_5_), channel_id=1, source_target_pairs={{0,4},{1,3},{2,6},{3,1},{4,0},{5,7},{6,2},{7,5},{8,12},{9,11},{10,... | collective-permute-start | bytes 393224 | tf_op jit(solution)/shard_map/ppermute | solution.py:211
  43.7 3.7 %gate_up_grad.6 = (bf16[12,20,128,128]{3,2,1,0:T(8,128)(2,1)}, bf16[12,20,128,128]{3,2,1,0:T(8,128)(2,1)}) custom-call(s32[13,20]{1,0:T(8,128)S(4)} %get-tuple-element.36.live_ref.refs_0_, bf16[65,32,128]{2,1,0:T(8,128)(2,1)S(1)} %get-tuple-element.44.refs_1_, ...), custom_call_target="tpu_custom_call", output_to_operand_aliasing={{0}: (3, {}), {1}: (4, {})} | custom-call | flops 251658240 | bytes 7864320 | tf_op jit(solution)/shard_map/gate_up_grad/pallas_call | solution.py:297
  47.4 0.1 collective-permute-done.10
  47.7 2.3 %collective-permute-start.11 = (bf16[2,2,8192]{2,1,0:T(2,128)(2,1)S(1)}, bf16[2,2,8192]{2,1,0:T(2,128)(2,1)S(1)}, u32[]{:S(2)}, u32[]{:S(2)}) collective-permute-start(bf16[2,2,8192]{2,1,0:T(2,128)(2,1)S(1)} %slice.75.refs_5_), channel_id=1, source_target_pairs={{0,8},{1,9},{2,10},{3,11},{4,12},{5,13},{6,14},{7,15},{8,0},{9,1},... | collective-permute-start | bytes 196616 | tf_op jit(solution)/shard_map/ppermute | solution.py:211
  50.0 2.8 %gate_up_grad.7 = (bf16[12,20,128,128]{3,2,1,0:T(8,128)(2,1)}, bf16[12,20,128,128]{3,2,1,0:T(8,128)(2,1)}) custom-call(s32[13,20]{1,0:T(8,128)S(4)} %get-tuple-element.36.live_ref.refs_0_, bf16[65,32,128]{2,1,0:T(8,128)(2,1)S(1)} %get-tuple-element.44.refs_1_, ...), custom_call_target="tpu_custom_call", output_to_operand_aliasing={{0}: (3, {}), {1}: (4, {})} | custom-call | flops 167772160 | bytes 5242880 | tf_op jit(solution)/shard_map/gate_up_grad/pallas_call | solution.py:297
  52.9 0.9 %collective-permute-done.11 = bf16[2,2,8192]{2,1,0:T(2,128)(2,1)S(1)} collective-permute-done((bf16[2,2,8192]{2,1,0:T(2,128)(2,1)S(1)}, bf16[2,2,8192]{2,1,0:T(2,128)(2,1)S(1)}, u32[]{:S(2)}, u32[]{:S(2)}) %collective-permute-start.11) | collective-permute-done | bytes 65568 | tf_op jit(solution)/shard_map/ppermute | solution.py:211
  53.9 0.7 %slice_bitcast_fusion = (bf16[2,8192]{1,0:T(2,128)(2,1)}, bf16[2,8192]{1,0:T(2,128)(2,1)}) fusion(bf16[2,2,8192]{2,1,0:T(2,128)(2,1)S(1)} %fusion), kind=kLoop, calls=%fused_computation.10 | loop fusion | bytes 131072 | tf_op jit(solution)/shard_map/squeeze | solution.py:336
  (23 shorter events, 1.4 us)
Async XLA Ops:
  0.6 6.6 %collective-permute-start.4 = (bf16[1,2,8192]{2,1,0:T(2,128)(2,1)}, bf16[1,2,8192]{2,1,0:T(2,128)(2,1)S(1)}, u32[]{:S(2)}, u32[]{:S(2)}) collective-permute-start(bf16[1,2,8192]{2,1,0:T(2,128)(2,1)} %bitcast.18), channel_id=1, source_target_pairs={{0,8},{1,9},{2,10},{3,11},{4,12},{5,13},{6,14},{7,15},{8,0},{9,1},... | collective-permute-start | bytes 98312 | tf_op jit(solution)/shard_map/ppermute | solution.py:211
  4.7 5.0 %collective-permute-start = (bf16[1,2,8192]{2,1,0:T(2,128)(2,1)}, bf16[1,2,8192]{2,1,0:T(2,128)(2,1)S(1)}, u32[]{:S(2)}, u32[]{:S(2)}) collective-permute-start(bf16[1,2,8192]{2,1,0:T(2,128)(2,1)} %bitcast.19), channel_id=1, source_target_pairs={{0,8},{1,9},{2,10},{3,11},{4,12},{5,13},{6,14},{7,15},{8,0},{9,1},... | collective-permute-start | bytes 98312 | tf_op jit(solution)/shard_map/ppermute | solution.py:211
  7.3 4.8 %collective-permute-start.5 = (bf16[2,2,8192]{2,1,0:T(2,128)(2,1)S(1)}, bf16[2,2,8192]{2,1,0:T(2,128)(2,1)S(1)}, u32[]{:S(2)}, u32[]{:S(2)}) collective-permute-start(bf16[2,2,8192]{2,1,0:T(2,128)(2,1)S(1)} %slice.53), channel_id=1, source_target_pairs={{0,2},{1,5},{2,0},{3,7},{4,6},{5,1},{6,4},{7,3},{8,10},{9,13},{10,... | collective-permute-start | bytes 196616 | tf_op jit(solution)/shard_map/ppermute | solution.py:211
  9.8 4.3 %collective-permute-start.1 = (bf16[2,2,8192]{2,1,0:T(2,128)(2,1)S(1)}, bf16[2,2,8192]{2,1,0:T(2,128)(2,1)S(1)}, u32[]{:S(2)}, u32[]{:S(2)}) collective-permute-start(bf16[2,2,8192]{2,1,0:T(2,128)(2,1)S(1)} %slice.51), channel_id=1, source_target_pairs={{0,4},{1,3},{2,6},{3,1},{4,0},{5,7},{6,2},{7,5},{8,12},{9,11},{10,... | collective-permute-start | bytes 196616 | tf_op jit(solution)/shard_map/ppermute | solution.py:211
  12.3 5.6 %collective-permute-start.6 = (bf16[4,2,8192]{2,1,0:T(2,128)(2,1)S(1)}, bf16[4,2,8192]{2,1,0:T(2,128)(2,1)S(1)}, u32[]{:S(2)}, u32[]{:S(2)}) collective-permute-start(bf16[4,2,8192]{2,1,0:T(2,128)(2,1)S(1)} %slice.54), channel_id=1, source_target_pairs={{0,4},{1,3},{2,6},{3,1},{4,0},{5,7},{6,2},{7,5},{8,12},{9,11},{10,... | collective-permute-start | bytes 393224 | tf_op jit(solution)/shard_map/ppermute | solution.py:211
  14.3 5.0 %collective-permute-start.2 = (bf16[4,2,8192]{2,1,0:T(2,128)(2,1)S(1)}, bf16[4,2,8192]{2,1,0:T(2,128)(2,1)S(1)}, u32[]{:S(2)}, u32[]{:S(2)}) collective-permute-start(bf16[4,2,8192]{2,1,0:T(2,128)(2,1)S(1)} %slice.52), channel_id=1, source_target_pairs={{0,2},{1,5},{2,0},{3,7},{4,6},{5,1},{6,4},{7,3},{8,10},{9,13},{10,... | collective-permute-start | bytes 393224 | tf_op jit(solution)/shard_map/ppermute | solution.py:211
  18.0 2.0 %collective-permute-start.7 = (bf16[8,2,8192]{2,1,0:T(2,128)(2,1)S(1)}, bf16[8,2,8192]{2,1,0:T(2,128)(2,1)S(1)}, u32[]{:S(2)}, u32[]{:S(2)}) collective-permute-start(bf16[8,2,8192]{2,1,0:T(2,128)(2,1)S(1)} %constant_dynamic-update-slice_fusion), channel_id=1, source_target_pairs={{0,1},{1,0},{2,3},{3,2},{4,5},{5,4},{6,7},{7,6},{8,9},{9,8},{10,11... | collective-permute-start | bytes 786440 | tf_op jit(solution)/shard_map/ppermute | solution.py:211
  19.5 1.6 %collective-permute-start.3 = (bf16[8,2,8192]{2,1,0:T(2,128)(2,1)S(1)}, bf16[8,2,8192]{2,1,0:T(2,128)(2,1)S(1)}, u32[]{:S(2)}, u32[]{:S(2)}) collective-permute-start(bf16[8,2,8192]{2,1,0:T(2,128)(2,1)S(1)} %constant_dynamic-update-slice_fusion.3), channel_id=1, source_target_pairs={{0,1},{1,0},{2,3},{3,2},{4,5},{5,4},{6,7},{7,6},{8,9},{9,8},{10,11... | collective-permute-start | bytes 786440 | tf_op jit(solution)/shard_map/ppermute | solution.py:211
  31.9 2.0 %collective-permute-start.8 = (bf16[2,16,8192]{2,1,0:T(8,128)(2,1)S(1)}, bf16[2,16,8192]{2,1,0:T(8,128)(2,1)S(1)}, u32[]{:S(2)}, u32[]{:S(2)}) collective-permute-start(bf16[2,16,8192]{2,1,0:T(8,128)(2,1)S(1)} %get-tuple-element.43), channel_id=1, source_target_pairs={{0,1},{1,0},{2,3},{3,2},{4,5},{5,4},{6,7},{7,6},{8,9},{9,8},{10,11... | collective-permute-start | bytes 1572872 | tf_op jit(solution)/shard_map/ppermute | solution.py:211
  34.0 8.3 %collective-permute-start.9 = (bf16[2,8,8192]{2,1,0:T(8,128)(2,1)S(1)}, bf16[2,8,8192]{2,1,0:T(8,128)(2,1)S(1)}, u32[]{:S(2)}, u32[]{:S(2)}) collective-permute-start(bf16[2,8,8192]{2,1,0:T(8,128)(2,1)S(1)} %slice.73.refs_5_.refs_3_), channel_id=1, source_target_pairs={{0,2},{1,5},{2,0},{3,7},{4,6},{5,1},{6,4},{7,3},{8,10},{9,13},{10,... | collective-permute-start | bytes 786440 | tf_op jit(solution)/shard_map/ppermute | solution.py:211
  42.5 5.0 %collective-permute-start.10 = (bf16[2,4,8192]{2,1,0:T(4,128)(2,1)S(1)}, bf16[2,4,8192]{2,1,0:T(4,128)(2,1)S(1)}, u32[]{:S(2)}, u32[]{:S(2)}) collective-permute-start(bf16[2,4,8192]{2,1,0:T(4,128)(2,1)S(1)} %slice.74.refs_5_), channel_id=1, source_target_pairs={{0,4},{1,3},{2,6},{3,1},{4,0},{5,7},{6,2},{7,5},{8,12},{9,11},{10,... | collective-permute-start | bytes 393224 | tf_op jit(solution)/shard_map/ppermute | solution.py:211
  47.7 6.1 %collective-permute-start.11 = (bf16[2,2,8192]{2,1,0:T(2,128)(2,1)S(1)}, bf16[2,2,8192]{2,1,0:T(2,128)(2,1)S(1)}, u32[]{:S(2)}, u32[]{:S(2)}) collective-permute-start(bf16[2,2,8192]{2,1,0:T(2,128)(2,1)S(1)} %slice.75.refs_5_), channel_id=1, source_target_pairs={{0,8},{1,9},{2,10},{3,11},{4,12},{5,13},{6,14},{7,15},{8,0},{9,1},... | collective-permute-start | bytes 196616 | tf_op jit(solution)/shard_map/ppermute | solution.py:211

commit v5 on v3

--- a/solution.py
+++ b/solution.py
@@ -9,7 +9,7 @@
 
 TN = (((0,), (0,)), ((), ()))
 CHUNK = 4
-STEP = 4
+STEP = 5
 LAG = 2
 
 

time: 54.5 us -> 54.6 us (level)
  starting transfers between devices: 15.2 us -> 18.5 us
  Pallas kernels: 26.1 us -> 24 us
  waiting for transfers between devices: 10 us -> 8.91 us
    ppermute x12, starting transfers between devices: 15.2 us -> 18.5 us  [swap(): return lax.ppermute(value, 'col', [(j, j ^ bits[j % 2]) for j in range(n)])]
    pallas_call x1, Pallas kernels: 12.6 us -> 10.5 us  [local(): pl.pallas_call(layer_kernel, in_specs=[smem] * 4 + [vmem] * 4 + [hbm] * 3...]
    ppermute x12, waiting for transfers between devices: 10 us -> 8.91 us  [swap(): return lax.ppermute(value, 'col', [(j, j ^ bits[j % 2]) for j in range(n)])]
  transfers between devices with their start and end apart: 12 -> 12, of which waited for: 10 -> 9; matrix products, arithmetic and copies ran while one was open for 2% -> 2% of each run, Pallas kernels for 25% -> 25%
where the time goes in v5:
time: 54.6 us; the launch traced here: 54.8 us
  Pallas kernels  24 us (44%)
  starting transfers between devices  18.5 us (34%)
  waiting for transfers between devices  8.91 us (16%)
  local copies, waits for them, and re-layouts  2.28 us (4%)
  between operations  0.85 us (2%)
    ppermute x12, starting transfers between devices, swap(): return lax.ppermute(value, 'col', [(j, j ^ bits[j % 2]) for j in range(n)])  18.5 us
    pallas_call x4, Pallas kernels, grads(): pl.pallas_call(functools.partial(grad_kernel, products, first, count, out...  12.1 us
    pallas_call x1, Pallas kernels, local(): pl.pallas_call(layer_kernel, in_specs=[smem] * 4 + [vmem] * 4 + [hbm] * 3...  10.5 us
    ppermute x12, waiting for transfers between devices, swap(): return lax.ppermute(value, 'col', [(j, j ^ bits[j % 2]) for j in range(n)])  8.91 us
    pallas_call x1, Pallas kernels, local(): pl.pallas_call(functools.partial(seed_kernel, width // blk), in_specs=[sm...  1.42 us
  transfers between devices with their start and end apart: 12, of which 9 were waited for; matrix products, arithmetic and copies ran while one was open for 2% of the time, Pallas kernels for 25%

profile of v5, /device:TPU:0, one launch (start us, length us, event | category | flops | bytes accessed | tf_op | source)
XLA Modules:
  0.0 54.8 jit_solution(17922678711070440661)
XLA Ops:
  0.6 4.1 %collective-permute-start.4 = (bf16[1,2,8192]{2,1,0:T(2,128)(2,1)}, bf16[1,2,8192]{2,1,0:T(2,128)(2,1)S(1)}, u32[]{:S(2)}, u32[]{:S(2)}) collective-permute-start(bf16[1,2,8192]{2,1,0:T(2,128)(2,1)} %bitcast.18), channel_id=1, source_target_pairs={{0,8},{1,9},{2,10},{3,11},{4,12},{5,13},{6,14},{7,15},{8,0},{9,1},... | collective-permute-start | bytes 98312 | tf_op jit(solution)/shard_map/ppermute | solution.py:211
  4.8 1.4 %seed.1 = (s32[13,20]{1,0:T(8,128)S(4)}, s32[70]{0:T(128)S(4)}, s32[70]{0:T(128)S(4)}, s32[1]{0:T(128)S(4)}, bf16[8,2,8192]{2,1,0:T(2,128)(2,1)S(1)}, /*index=5*/bf16[8,2,8192]{2,1,0:T(2,128)(2,1)S(1)}) custom-call(s32[12,20]{1,0:T(8,128)} %rows_ref.1, s32[12]{0:T(128)} %count_ref.1, bf16[2,8192]{1,0:T(2,128)(2,1)} %x_ref.1, bf16[2,8192]{1,0:T(2,128)(2,1)} %dy_ref.1), custom_call_target="tpu_custom_call" | custom-call | tf_op jit(solution)/shard_map/seed/pallas_call | solution.py:250
  6.2 1.0 %collective-permute-done.4 = bf16[1,2,8192]{2,1,0:T(2,128)(2,1)S(1)} collective-permute-done((bf16[1,2,8192]{2,1,0:T(2,128)(2,1)}, bf16[1,2,8192]{2,1,0:T(2,128)(2,1)S(1)}, u32[]{:S(2)}, u32[]{:S(2)}) %collective-permute-start.4) | collective-permute-done | bytes 32800 | tf_op jit(solution)/shard_map/ppermute | solution.py:211
  7.3 1.8 %collective-permute-start.5 = (bf16[2,2,8192]{2,1,0:T(2,128)(2,1)S(1)}, bf16[2,2,8192]{2,1,0:T(2,128)(2,1)S(1)}, u32[]{:S(2)}, u32[]{:S(2)}) collective-permute-start(bf16[2,2,8192]{2,1,0:T(2,128)(2,1)S(1)} %slice.53), channel_id=1, source_target_pairs={{0,2},{1,5},{2,0},{3,7},{4,6},{5,1},{6,4},{7,3},{8,10},{9,13},{10,... | collective-permute-start | bytes 196616 | tf_op jit(solution)/shard_map/ppermute | solution.py:211
  9.1 0.7 %collective-permute-done = bf16[1,2,8192]{2,1,0:T(2,128)(2,1)S(1)} collective-permute-done((bf16[1,2,8192]{2,1,0:T(2,128)(2,1)}, bf16[1,2,8192]{2,1,0:T(2,128)(2,1)S(1)}, u32[]{:S(2)}, u32[]{:S(2)}) %collective-permute-start) | collective-permute-done | bytes 32800 | tf_op jit(solution)/shard_map/ppermute | solution.py:211
  9.8 1.6 %collective-permute-start.1 = (bf16[2,2,8192]{2,1,0:T(2,128)(2,1)S(1)}, bf16[2,2,8192]{2,1,0:T(2,128)(2,1)S(1)}, u32[]{:S(2)}, u32[]{:S(2)}) collective-permute-start(bf16[2,2,8192]{2,1,0:T(2,128)(2,1)S(1)} %slice.51), channel_id=1, source_target_pairs={{0,4},{1,3},{2,6},{3,1},{4,0},{5,7},{6,2},{7,5},{8,12},{9,11},{10,... | collective-permute-start | bytes 196616 | tf_op jit(solution)/shard_map/ppermute | solution.py:211
  11.5 0.6 %collective-permute-done.5 = bf16[2,2,8192]{2,1,0:T(2,128)(2,1)S(1)} collective-permute-done((bf16[2,2,8192]{2,1,0:T(2,128)(2,1)S(1)}, bf16[2,2,8192]{2,1,0:T(2,128)(2,1)S(1)}, u32[]{:S(2)}, u32[]{:S(2)}) %collective-permute-start.5) | collective-permute-done | bytes 65568 | tf_op jit(solution)/shard_map/ppermute | solution.py:211
  12.3 1.8 %collective-permute-start.6 = (bf16[4,2,8192]{2,1,0:T(2,128)(2,1)S(1)}, bf16[4,2,8192]{2,1,0:T(2,128)(2,1)S(1)}, u32[]{:S(2)}, u32[]{:S(2)}) collective-permute-start(bf16[4,2,8192]{2,1,0:T(2,128)(2,1)S(1)} %slice.54), channel_id=1, source_target_pairs={{0,4},{1,3},{2,6},{3,1},{4,0},{5,7},{6,2},{7,5},{8,12},{9,11},{10,... | collective-permute-start | bytes 393224 | tf_op jit(solution)/shard_map/ppermute | solution.py:211
  14.3 1.6 %collective-permute-start.2 = (bf16[4,2,8192]{2,1,0:T(2,128)(2,1)S(1)}, bf16[4,2,8192]{2,1,0:T(2,128)(2,1)S(1)}, u32[]{:S(2)}, u32[]{:S(2)}) collective-permute-start(bf16[4,2,8192]{2,1,0:T(2,128)(2,1)S(1)} %slice.52), channel_id=1, source_target_pairs={{0,2},{1,5},{2,0},{3,7},{4,6},{5,1},{6,4},{7,3},{8,10},{9,13},{10,... | collective-permute-start | bytes 393224 | tf_op jit(solution)/shard_map/ppermute | solution.py:211
  15.9 1.9 %collective-permute-done.6 = bf16[4,2,8192]{2,1,0:T(2,128)(2,1)S(1)} collective-permute-done((bf16[4,2,8192]{2,1,0:T(2,128)(2,1)S(1)}, bf16[4,2,8192]{2,1,0:T(2,128)(2,1)S(1)}, u32[]{:S(2)}, u32[]{:S(2)}) %collective-permute-start.6) | collective-permute-done | bytes 131104 | tf_op jit(solution)/shard_map/ppermute | solution.py:211
  17.9 0.1 constant_dynamic-update-slice_fusion
  18.0 1.3 %collective-permute-done.2 = bf16[4,2,8192]{2,1,0:T(2,128)(2,1)S(1)} collective-permute-done((bf16[4,2,8192]{2,1,0:T(2,128)(2,1)S(1)}, bf16[4,2,8192]{2,1,0:T(2,128)(2,1)S(1)}, u32[]{:S(2)}, u32[]{:S(2)}) %collective-permute-start.2) | collective-permute-done | bytes 131104 | tf_op jit(solution)/shard_map/ppermute | solution.py:211
  19.4 0.1 constant_dynamic-update-slice_fusion.3
  19.6 0.1 reshape.28.x_near
  19.7 0.2 copy.21
  19.9 0.1 reshape.31.dy_near
  20.0 0.2 copy.20
  20.2 0.1 reshape.33.dy_far
  20.3 0.8 %collective-permute-done.3 = bf16[8,2,8192]{2,1,0:T(2,128)(2,1)S(1)} collective-permute-done((bf16[8,2,8192]{2,1,0:T(2,128)(2,1)S(1)}, bf16[8,2,8192]{2,1,0:T(2,128)(2,1)S(1)}, u32[]{:S(2)}, u32[]{:S(2)}) %collective-permute-start.3) | collective-permute-done | bytes 262176 | tf_op jit(solution)/shard_map/ppermute | solution.py:211
  21.1 0.1 reshape.29.x_far
  21.2 10.5 %layer.1 = (bf16[13,32,128]{2,1,0:T(8,128)(2,1)S(1)}, bf16[13,32,256]{2,1,0:T(8,128)(2,1)S(1)}, bf16[65,32,128]{2,1,0:T(8,128)(2,1)S(1)}, bf16[65,32,128]{2,1,0:...) custom-call(s32[13,20]{1,0:T(8,128)S(4)} %get-tuple-element.31.live_ref.refs_0_, ...), custom_call_target="tpu_custom_call" | custom-call | flops 1509949440 | bytes 23592960 | tf_op jit(solution)/shard_map/layer/pallas_call | solution.py:273
  31.7 1.8 %collective-permute-start.8 = (bf16[2,16,8192]{2,1,0:T(8,128)(2,1)S(1)}, bf16[2,16,8192]{2,1,0:T(8,128)(2,1)S(1)}, u32[]{:S(2)}, u32[]{:S(2)}) collective-permute-start(bf16[2,16,8192]{2,1,0:T(8,128)(2,1)S(1)} %get-tuple-element.38), channel_id=1, source_target_pairs={{0,1},{1,0},{2,3},{3,2},{4,5},{5,4},{6,7},{7,6},{8,9},{9,8},{10,11... | collective-permute-start | bytes 1572872 | tf_op jit(solution)/shard_map/ppermute | solution.py:211
  33.5 1.9 %gate_up_grad.3 = (bf16[12,20,128,128]{3,2,1,0:T(8,128)(2,1)}, bf16[12,20,128,128]{3,2,1,0:T(8,128)(2,1)}) custom-call(s32[13,20]{1,0:T(8,128)S(4)} %get-tuple-element.31.live_ref.refs_0_, bf16[65,32,128]{2,1,0:T(8,128)(2,1)S(1)} %get-tuple-element.39.refs_1_, bf16[13,32,256]{2,1,0:T(8,128)(2,1)S(1)} %get-tuple-element.40.refs_2_), custom_call_target="tpu_custom_call" | custom-call | flops 83886080 | bytes 2621440 | tf_op jit(solution)/shard_map/gate_up_grad/pallas_call | solution.py:297
  35.6 1.2 %collective-permute-start.9 = (bf16[2,8,8192]{2,1,0:T(8,128)(2,1)S(1)}, bf16[2,8,8192]{2,1,0:T(8,128)(2,1)S(1)}, u32[]{:S(2)}, u32[]{:S(2)}) collective-permute-start(bf16[2,8,8192]{2,1,0:T(8,128)(2,1)S(1)} %slice.73.refs_3_), channel_id=1, source_target_pairs={{0,2},{1,5},{2,0},{3,7},{4,6},{5,1},{6,4},{7,3},{8,10},{9,13},{10,... | collective-permute-start | bytes 786440 | tf_op jit(solution)/shard_map/ppermute | solution.py:211
  36.8 3.6 %down_grad.1 = bf16[12,20,128,128]{3,2,1,0:T(8,128)(2,1)} custom-call(s32[13,20]{1,0:T(8,128)S(4)} %get-tuple-element.31.live_ref.refs_0_, bf16[65,32,128]{2,1,0:T(8,128)(2,1)S(1)} %get-tuple-element.44.refs_1_, bf16[13,32,128]{2,1,0:T(8,128)(2,1)S(1)} %get-tuple-element.45.refs_2_, bf16[2,8,8192]{2,1,0:T(8,128)(2,1)S(1)} %slice.73.refs_3_), custom_call_target="tpu_custom_call" | custom-call | flops 251658240 | bytes 7864320 | tf_op jit(solution)/shard_map/down_grad/pallas_call | solution.py:297
  40.5 1.6 %collective-permute-done.9 = bf16[2,8,8192]{2,1,0:T(8,128)(2,1)S(1)} collective-permute-done((bf16[2,8,8192]{2,1,0:T(8,128)(2,1)S(1)}, bf16[2,8,8192]{2,1,0:T(8,128)(2,1)S(1)}, u32[]{:S(2)}, u32[]{:S(2)}) %collective-permute-start.9) | collective-permute-done | bytes 262176 | tf_op jit(solution)/shard_map/ppermute | solution.py:211
  42.2 1.6 %collective-permute-start.10 = (bf16[2,4,8192]{2,1,0:T(4,128)(2,1)S(1)}, bf16[2,4,8192]{2,1,0:T(4,128)(2,1)S(1)}, u32[]{:S(2)}, u32[]{:S(2)}) collective-permute-start(bf16[2,4,8192]{2,1,0:T(4,128)(2,1)S(1)} %slice.74.refs_5_), channel_id=1, source_target_pairs={{0,4},{1,3},{2,6},{3,1},{4,0},{5,7},{6,2},{7,5},{8,12},{9,11},{10,... | collective-permute-start | bytes 393224 | tf_op jit(solution)/shard_map/ppermute | solution.py:211
  43.8 3.7 %gate_up_grad.4 = (bf16[12,20,128,128]{3,2,1,0:T(8,128)(2,1)}, bf16[12,20,128,128]{3,2,1,0:T(8,128)(2,1)}) custom-call(s32[13,20]{1,0:T(8,128)S(4)} %get-tuple-element.31.live_ref.refs_0_, bf16[65,32,128]{2,1,0:T(8,128)(2,1)S(1)} %get-tuple-element.39.refs_1_, ...), custom_call_target="tpu_custom_call", output_to_operand_aliasing={{0}: (3, {}), {1}: (4, {})} | custom-call | flops 251658240 | bytes 7864320 | tf_op jit(solution)/shard_map/gate_up_grad/pallas_call | solution.py:297
  47.6 2.6 %collective-permute-start.11 = (bf16[2,2,8192]{2,1,0:T(2,128)(2,1)S(1)}, bf16[2,2,8192]{2,1,0:T(2,128)(2,1)S(1)}, u32[]{:S(2)}, u32[]{:S(2)}) collective-permute-start(bf16[2,2,8192]{2,1,0:T(2,128)(2,1)S(1)} %slice.75.refs_5_), channel_id=1, source_target_pairs={{0,8},{1,9},{2,10},{3,11},{4,12},{5,13},{6,14},{7,15},{8,0},{9,1},... | collective-permute-start | bytes 196616 | tf_op jit(solution)/shard_map/ppermute | solution.py:211
  50.3 2.8 %gate_up_grad.5 = (bf16[12,20,128,128]{3,2,1,0:T(8,128)(2,1)}, bf16[12,20,128,128]{3,2,1,0:T(8,128)(2,1)}) custom-call(s32[13,20]{1,0:T(8,128)S(4)} %get-tuple-element.31.live_ref.refs_0_, bf16[65,32,128]{2,1,0:T(8,128)(2,1)S(1)} %get-tuple-element.39.refs_1_, ...), custom_call_target="tpu_custom_call", output_to_operand_aliasing={{0}: (3, {}), {1}: (4, {})} | custom-call | flops 167772160 | bytes 5242880 | tf_op jit(solution)/shard_map/gate_up_grad/pallas_call | solution.py:297
  53.1 0.9 %collective-permute-done.11 = bf16[2,2,8192]{2,1,0:T(2,128)(2,1)S(1)} collective-permute-done((bf16[2,2,8192]{2,1,0:T(2,128)(2,1)S(1)}, bf16[2,2,8192]{2,1,0:T(2,128)(2,1)S(1)}, u32[]{:S(2)}, u32[]{:S(2)}) %collective-permute-start.11) | collective-permute-done | bytes 65568 | tf_op jit(solution)/shard_map/ppermute | solution.py:211
  54.1 0.7 %slice_bitcast_fusion = (bf16[2,8192]{1,0:T(2,128)(2,1)}, bf16[2,8192]{1,0:T(2,128)(2,1)}) fusion(bf16[2,2,8192]{2,1,0:T(2,128)(2,1)S(1)} %fusion), kind=kLoop, calls=%fused_computation.10 | loop fusion | bytes 131072 | tf_op jit(solution)/shard_map/squeeze | solution.py:341
  (22 shorter events, 1.2 us)
Async XLA Ops:
  0.6 6.6 %collective-permute-start.4 = (bf16[1,2,8192]{2,1,0:T(2,128)(2,1)}, bf16[1,2,8192]{2,1,0:T(2,128)(2,1)S(1)}, u32[]{:S(2)}, u32[]{:S(2)}) collective-permute-start(bf16[1,2,8192]{2,1,0:T(2,128)(2,1)} %bitcast.18), channel_id=1, source_target_pairs={{0,8},{1,9},{2,10},{3,11},{4,12},{5,13},{6,14},{7,15},{8,0},{9,1},... | collective-permute-start | bytes 98312 | tf_op jit(solution)/shard_map/ppermute | solution.py:211
  4.7 5.0 %collective-permute-start = (bf16[1,2,8192]{2,1,0:T(2,128)(2,1)}, bf16[1,2,8192]{2,1,0:T(2,128)(2,1)S(1)}, u32[]{:S(2)}, u32[]{:S(2)}) collective-permute-start(bf16[1,2,8192]{2,1,0:T(2,128)(2,1)} %bitcast.19), channel_id=1, source_target_pairs={{0,8},{1,9},{2,10},{3,11},{4,12},{5,13},{6,14},{7,15},{8,0},{9,1},... | collective-permute-start | bytes 98312 | tf_op jit(solution)/shard_map/ppermute | solution.py:211
  7.3 4.8 %collective-permute-start.5 = (bf16[2,2,8192]{2,1,0:T(2,128)(2,1)S(1)}, bf16[2,2,8192]{2,1,0:T(2,128)(2,1)S(1)}, u32[]{:S(2)}, u32[]{:S(2)}) collective-permute-start(bf16[2,2,8192]{2,1,0:T(2,128)(2,1)S(1)} %slice.53), channel_id=1, source_target_pairs={{0,2},{1,5},{2,0},{3,7},{4,6},{5,1},{6,4},{7,3},{8,10},{9,13},{10,... | collective-permute-start | bytes 196616 | tf_op jit(solution)/shard_map/ppermute | solution.py:211
  9.8 4.3 %collective-permute-start.1 = (bf16[2,2,8192]{2,1,0:T(2,128)(2,1)S(1)}, bf16[2,2,8192]{2,1,0:T(2,128)(2,1)S(1)}, u32[]{:S(2)}, u32[]{:S(2)}) collective-permute-start(bf16[2,2,8192]{2,1,0:T(2,128)(2,1)S(1)} %slice.51), channel_id=1, source_target_pairs={{0,4},{1,3},{2,6},{3,1},{4,0},{5,7},{6,2},{7,5},{8,12},{9,11},{10,... | collective-permute-start | bytes 196616 | tf_op jit(solution)/shard_map/ppermute | solution.py:211
  12.3 5.6 %collective-permute-start.6 = (bf16[4,2,8192]{2,1,0:T(2,128)(2,1)S(1)}, bf16[4,2,8192]{2,1,0:T(2,128)(2,1)S(1)}, u32[]{:S(2)}, u32[]{:S(2)}) collective-permute-start(bf16[4,2,8192]{2,1,0:T(2,128)(2,1)S(1)} %slice.54), channel_id=1, source_target_pairs={{0,4},{1,3},{2,6},{3,1},{4,0},{5,7},{6,2},{7,5},{8,12},{9,11},{10,... | collective-permute-start | bytes 393224 | tf_op jit(solution)/shard_map/ppermute | solution.py:211
  14.3 5.0 %collective-permute-start.2 = (bf16[4,2,8192]{2,1,0:T(2,128)(2,1)S(1)}, bf16[4,2,8192]{2,1,0:T(2,128)(2,1)S(1)}, u32[]{:S(2)}, u32[]{:S(2)}) collective-permute-start(bf16[4,2,8192]{2,1,0:T(2,128)(2,1)S(1)} %slice.52), channel_id=1, source_target_pairs={{0,2},{1,5},{2,0},{3,7},{4,6},{5,1},{6,4},{7,3},{8,10},{9,13},{10,... | collective-permute-start | bytes 393224 | tf_op jit(solution)/shard_map/ppermute | solution.py:211
  18.0 2.0 %collective-permute-start.7 = (bf16[8,2,8192]{2,1,0:T(2,128)(2,1)S(1)}, bf16[8,2,8192]{2,1,0:T(2,128)(2,1)S(1)}, u32[]{:S(2)}, u32[]{:S(2)}) collective-permute-start(bf16[8,2,8192]{2,1,0:T(2,128)(2,1)S(1)} %constant_dynamic-update-slice_fusion), channel_id=1, source_target_pairs={{0,1},{1,0},{2,3},{3,2},{4,5},{5,4},{6,7},{7,6},{8,9},{9,8},{10,11... | collective-permute-start | bytes 786440 | tf_op jit(solution)/shard_map/ppermute | solution.py:211
  19.5 1.6 %collective-permute-start.3 = (bf16[8,2,8192]{2,1,0:T(2,128)(2,1)S(1)}, bf16[8,2,8192]{2,1,0:T(2,128)(2,1)S(1)}, u32[]{:S(2)}, u32[]{:S(2)}) collective-permute-start(bf16[8,2,8192]{2,1,0:T(2,128)(2,1)S(1)} %constant_dynamic-update-slice_fusion.3), channel_id=1, source_target_pairs={{0,1},{1,0},{2,3},{3,2},{4,5},{5,4},{6,7},{7,6},{8,9},{9,8},{10,11... | collective-permute-start | bytes 786440 | tf_op jit(solution)/shard_map/ppermute | solution.py:211
  31.7 3.8 %collective-permute-start.8 = (bf16[2,16,8192]{2,1,0:T(8,128)(2,1)S(1)}, bf16[2,16,8192]{2,1,0:T(8,128)(2,1)S(1)}, u32[]{:S(2)}, u32[]{:S(2)}) collective-permute-start(bf16[2,16,8192]{2,1,0:T(8,128)(2,1)S(1)} %get-tuple-element.38), channel_id=1, source_target_pairs={{0,1},{1,0},{2,3},{3,2},{4,5},{5,4},{6,7},{7,6},{8,9},{9,8},{10,11... | collective-permute-start | bytes 1572872 | tf_op jit(solution)/shard_map/ppermute | solution.py:211
  35.6 6.4 %collective-permute-start.9 = (bf16[2,8,8192]{2,1,0:T(8,128)(2,1)S(1)}, bf16[2,8,8192]{2,1,0:T(8,128)(2,1)S(1)}, u32[]{:S(2)}, u32[]{:S(2)}) collective-permute-start(bf16[2,8,8192]{2,1,0:T(8,128)(2,1)S(1)} %slice.73.refs_3_), channel_id=1, source_target_pairs={{0,2},{1,5},{2,0},{3,7},{4,6},{5,1},{6,4},{7,3},{8,10},{9,13},{10,... | collective-permute-start | bytes 786440 | tf_op jit(solution)/shard_map/ppermute | solution.py:211
  42.2 5.3 %collective-permute-start.10 = (bf16[2,4,8192]{2,1,0:T(4,128)(2,1)S(1)}, bf16[2,4,8192]{2,1,0:T(4,128)(2,1)S(1)}, u32[]{:S(2)}, u32[]{:S(2)}) collective-permute-start(bf16[2,4,8192]{2,1,0:T(4,128)(2,1)S(1)} %slice.74.refs_5_), channel_id=1, source_target_pairs={{0,4},{1,3},{2,6},{3,1},{4,0},{5,7},{6,2},{7,5},{8,12},{9,11},{10,... | collective-permute-start | bytes 393224 | tf_op jit(solution)/shard_map/ppermute | solution.py:211
  47.6 6.4 %collective-permute-start.11 = (bf16[2,2,8192]{2,1,0:T(2,128)(2,1)S(1)}, bf16[2,2,8192]{2,1,0:T(2,128)(2,1)S(1)}, u32[]{:S(2)}, u32[]{:S(2)}) collective-permute-start(bf16[2,2,8192]{2,1,0:T(2,128)(2,1)S(1)} %slice.75.refs_5_), channel_id=1, source_target_pairs={{0,8},{1,9},{2,10},{3,11},{4,12},{5,13},{6,14},{7,15},{8,0},{9,1},... | collective-permute-start | bytes 196616 | tf_op jit(solution)/shard_map/ppermute | solution.py:211
